TPU v7x, 256 devices: a whole 4x4x8 slice. The times are simulated.
256 devices in a mesh: lat: 64 (over z, y, core), ch: 4 (over x).
Axes of the slice: x: 4, y: 4, z: 8, core: 2. Of those that a mesh axis runs over, the one named last changes fastest.
Arguments:
- grid: bfloat16 [512, 1440, 512], P('lat', None, 'ch'), may hold values from -6 to 6
- legendre: bfloat16 [384, 384, 512], P('lat'), may hold values from -1 to 1, as said below
- m_order: int32 [384], replicated, may hold values from 0 to 383, as said below
- quad_weights: float32 [512], replicated, may hold values from 0.5 to 1.5
- mix_real: bfloat16 [512, 512], replicated, may hold values from -0.1875 to 0.1875
- mix_imag: bfloat16 [512, 512], replicated, may hold values from -0.1875 to 0.1875
- spec_gain: float32 [384, 512], replicated, may hold values from 0.5 to 2
- ln_gain: float32 [512], replicated, may hold values from 0.5 to 1.5
- mlp_in: bfloat16 [512, 1024], replicated, may hold values from -0.25 to 0.25
- mlp_bias: float32 [1024], replicated, may hold values from -3 to 3
- mlp_out: bfloat16 [1024, 512], replicated, may hold values from -0.1875 to 0.1875
Outputs:
- block_out: bfloat16 [512, 1440, 512], P('lat', 'ch')
Inputs may be any that keep to these rules, and one draw needn't show every extreme that they name: `m_order`: a permutation of 0 to 383. legendre[r, l, cycle] is zero wherever l < m_order[r].
All inputs are finite; a program needn't handle non-finite values.
Results may differ from a plain program's by a relative error of at most 0.013.
Values may be sent and summed in bfloat16 or wider, within the bound.
A program may use at most 64 MiB of HBM per device.

v0:
```python
import math

import jax
import jax.numpy as jnp
from jax import lax
from jax.sharding import PartitionSpec as P


def forward_tables(order, nlon):
    steps = jnp.arange(nlon, dtype=jnp.int32)
    index = steps[:, None] * order[None, :] % nlon
    angle = index.astype(jnp.float32) * (2.0 * math.pi / nlon)
    scale = 1.0 / math.sqrt(nlon)
    return (
        (jnp.cos(angle) * scale).astype(jnp.bfloat16),
        (-jnp.sin(angle) * scale).astype(jnp.bfloat16),
    )


def inverse_tables(order, nlon):
    steps = jnp.arange(nlon, dtype=jnp.int32)
    index = order[:, None] * steps[None, :] % nlon
    angle = index.astype(jnp.float32) * (2.0 * math.pi / nlon)
    factor = jnp.where(order == 0, 1.0, 2.0).astype(jnp.float32)[:, None] / math.sqrt(nlon)
    return (
        (jnp.cos(angle) * factor).astype(jnp.bfloat16),
        (-jnp.sin(angle) * factor).astype(jnp.bfloat16),
    )


def point_layer(rows, ln_gain, mlp_in, mlp_bias, mlp_out):
    values = rows.astype(jnp.float32)
    center = jnp.mean(values, axis=-1, keepdims=True)
    spread = jnp.mean((values - center) ** 2, axis=-1, keepdims=True)
    normed = ((values - center) * lax.rsqrt(spread + 1e-05) * ln_gain).astype(jnp.bfloat16)
    inner = jnp.dot(normed, mlp_in, preferred_element_type=jnp.float32) + mlp_bias
    hidden = jax.nn.gelu(inner, approximate=True).astype(jnp.bfloat16)
    return (values + jnp.dot(hidden, mlp_out, preferred_element_type=jnp.float32)).astype(
        jnp.bfloat16
    )


def body(
    grid,
    legendre,
    m_order,
    quad_weights,
    mix_real,
    mix_imag,
    spec_gain,
    ln_gain,
    mlp_in,
    mlp_bias,
    mlp_out,
):
    cycle_count, nlon, chans = grid.shape
    fwd_cos, fwd_sin = forward_tables(m_order, nlon)
    real_part = jnp.einsum("lnc,nm->mlc", grid, fwd_cos, preferred_element_type=jnp.float32)
    imag_part = jnp.einsum("lnc,nm->mlc", grid, fwd_sin, preferred_element_type=jnp.float32)
    spectra = jnp.stack([real_part, imag_part], axis=2).astype(jnp.bfloat16)
    weighted = (legendre * quad_weights[None, None, :]).astype(jnp.bfloat16)
    totals = jnp.einsum(
        "mln,mnjc->mljc",
        weighted,
        lax.all_to_all(spectra, "lat", split_axis=0, concat_axis=1, tiled=True),
        preferred_element_type=jnp.float32,
    )
    coeffs = totals.astype(jnp.bfloat16)
    coef_re = coeffs[:, :, 0, :]
    coef_im = coeffs[:, :, 1, :]
    offset = lax.axis_index("ch") * chans
    cols_re = lax.dynamic_slice_in_dim(mix_real, offset, chans, 1)
    cols_im = lax.dynamic_slice_in_dim(mix_imag, offset, chans, 1)
    gain_cols = lax.dynamic_slice_in_dim(spec_gain, offset, chans, 1)
    pieces = (
        lax.all_gather(coef_re, "ch", axis=2, tiled=True),
        lax.all_gather(coef_im, "ch", axis=2, tiled=True),
    )
    new_re = jnp.einsum(
        "mlc,cd->mld", pieces[0], cols_re, preferred_element_type=jnp.float32
    ) - jnp.einsum("mlc,cd->mld", pieces[1], cols_im, preferred_element_type=jnp.float32)
    new_im = jnp.einsum(
        "mlc,cd->mld", pieces[0], cols_im, preferred_element_type=jnp.float32
    ) + jnp.einsum("mlc,cd->mld", pieces[1], cols_re, preferred_element_type=jnp.float32)
    filtered = jnp.stack([new_re * gain_cols[None], new_im * gain_cols[None]], axis=2).astype(
        jnp.bfloat16
    )
    back = jnp.einsum("mln,mljc->mnjc", legendre, filtered, preferred_element_type=jnp.float32)
    back = back.astype(jnp.bfloat16)
    inv_cos, inv_sin = inverse_tables(m_order, nlon)
    block = lax.all_to_all(back, "lat", split_axis=1, concat_axis=0, tiled=True)
    wave = jnp.einsum("mlc,mn->lnc", block[:, :, 0, :], inv_cos, preferred_element_type=jnp.float32)
    waves = wave + jnp.einsum(
        "mlc,mn->lnc", block[:, :, 1, :], inv_sin, preferred_element_type=jnp.float32
    )
    summed = (grid.astype(jnp.float32) + waves).astype(jnp.bfloat16)
    block = lax.all_to_all(summed, "ch", split_axis=1, concat_axis=2, tiled=True)
    rows = block.reshape(-1, block.shape[2])
    result = point_layer(rows, ln_gain, mlp_in, mlp_bias, mlp_out)
    return result.reshape(block.shape)


def solution(mesh):
    placed = (
        P("lat", None, "ch"),
        P("lat", None, None),
        P(),
        P(),
        P(),
        P(),
        P(),
        P(),
        P(),
        P(),
        P(),
    )
    return jax.shard_map(
        body, mesh=mesh, in_specs=placed, out_specs=P("lat", "ch", None), check_vma=False
    )
```

profile of v0, /device:TPU:16, one launch (start us, length us, event | category | flops | bytes accessed | tf_op | source)
XLA Modules:
  0.0 366.5 jit_solution(8324836321965757253)
XLA Ops:
  6.5 0.0 copy-start
  6.5 11.4 %fusion.87 = bf16[384,8,1,128]{3,0,1,2:T(8,128)(2,1)S(1)} fusion(bf16[8,1440,128]{2,1,0:T(8,128)(2,1)} %param.11, s32[384]{0:T(512)} %param.13), kind=kOutput, calls=%fused_computation.74 | convolution fusion | flops 1139490816 | bytes 3737088 | tf_op jit(solution)/shard_map/lnc,nm->mlc/dot_general | solution.py:59
  18.0 0.0 copy-done.5
  18.0 0.0 copy-done.6
  18.0 10.1 %fusion.86 = bf16[384,8,1,128]{3,0,1,2:T(8,128)(2,1)S(1)} fusion(bf16[8,1440,128]{2,1,0:T(8,128)(2,1)S(1)} %copy-done.6, s32[384]{0:T(512)S(1)} %copy-done.5), kind=kOutput, calls=%fused_computation.73 | convolution fusion | flops 1138937856 | bytes 3737088 | tf_op jit(solution)/shard_map/lnc,nm->mlc/dot_general | solution.py:58
  28.1 0.1 pad_maximum_fusion
  28.2 1.0 copy.24
  29.3 0.0 copy-start.8
  29.3 0.0 copy-start.12
  29.3 52.0 %all_to_all.45 = bf16[384,8,2,128]{3,1,2,0:T(8,128)(2,1)S(1)} all-to-all(bf16[384,8,2,128]{3,1,2,0:T(8,128)(2,1)S(1)} %copy.24), channel_id=1, replica_groups=mesh['lat'=64,'ch'=4] {'lat'}, dimensions={0} | all-to-all | bytes 3145728 | tf_op jit(solution)/shard_map/all_to_all | solution.py:65
  81.2 0.0 copy-done.12
  81.2 0.8 fusion.60
  82.0 1.1 fusion.155
  83.1 0.0 all-gather.7.cloned.1.call-update
  83.2 0.0 all-gather.5.cloned.1.call-start
  83.2 0.7 all-gather.5.cloned.1.call-update
  83.9 1.6 constant_dynamic-slice_fusion
  85.5 33.2 %all-gather.7.cloned.1.call-done = bf16[6,384,1,512]{3,1,2,0:T(8,128)(2,1)} async-done(((bf16[6,384,1,128]{3,1,2,0:T(8,128)(2,1)}), bf16[6,384,1,512]{3,1,2,0:T(8,128)(2,1)}) %all-gather.7.cloned.1.call-update) | async-done | bytes 2359312 | tf_op jit(solution)/shard_map/all_gather | solution.py:77
  118.7 2.6 fusion.36
  121.3 1.7 fusion.38
  123.0 37.8 %all-gather.5.cloned.1.call-done = bf16[6,384,1,512]{3,1,2,0:T(8,128)(2,1)} async-done(((bf16[6,384,1,128]{3,1,2,0:T(8,128)(2,1)}), bf16[6,384,1,512]{3,1,2,0:T(8,128)(2,1)}) %all-gather.5.cloned.1.call-update) | async-done | bytes 2359312 | tf_op jit(solution)/shard_map/all_gather | solution.py:76
  160.8 2.7 fusion.88
  163.4 0.0 copy-start.9
  163.5 1.9 fusion.91
  165.4 1.0 fusion.65
  166.4 2.9 copy.27
  169.3 10.9 %all-to-all-start.1 = ((bf16[6,512,2,128]{3,2,0,1:T(2,128)(2,1)}), bf16[6,512,2,128]{3,2,0,1:T(2,128)(2,1)S(1)}, u32[]{:S(2)}, u32[]{:S(2)}) async-start(bf16[6,512,2,128]{3,2,0,1:T(2,128)(2,1)} %copy.27), calls=%async_computation.1 | async-start | bytes 3145728 | tf_op jit(solution)/shard_map/all_to_all | solution.py:91
  180.1 39.9 %all-to-all-done.1 = bf16[6,512,2,128]{3,2,0,1:T(2,128)(2,1)S(1)} async-done(((bf16[6,512,2,128]{3,2,0,1:T(2,128)(2,1)}), bf16[6,512,2,128]{3,2,0,1:T(2,128)(2,1)S(1)}, u32[]{:S(2)}, u32[]{:S(2)}) %all-to-all-start.1) | async-done | bytes 1572896 | tf_op jit(solution)/shard_map/all_to_all | solution.py:91
  220.0 0.2 copy.63
  220.3 0.3 copy.29
  220.6 0.1 fusion.154
  220.7 0.0 copy-start.7
  220.7 9.6 %fusion.100 = f32[1440,8,128]{2,0,1:T(8,128)S(1)} fusion(f32[384]{0:T(512)S(1)} %select_multiply_fusion, s32[384]{0:T(512)S(1)} %copy-done.5, bf16[384,8,1,128]{3,1,2,0:T(8,128)(2,1)S(1)} %get-tuple-element.6), kind=kOutput, calls=%fused_computation.83 | convolution fusion | flops 1138544640 | bytes 6687744 | tf_op jit(solution)/shard_map/mlc,mn->lnc/dot_general | solution.py:92
  230.3 10.8 %fusion.14 = bf16[8,1440,128]{2,1,0:T(8,128)(2,1)S(1)} fusion(f32[1440,8,128]{2,0,1:T(8,128)S(1)} %fusion.100, bf16[8,1440,128]{2,1,0:T(8,128)(2,1)S(1)} %copy-done.7, f32[384]{0:T(512)S(1)} %select_multiply_fusion, s32[384]{0:T(512)S(1)} %copy-done.5, bf16[384,8,1,128]{3,1,2,0:T(8,128)(2,1)S(1)} %get-tuple-element.5), kind=kOutput, calls=%fused_computation.20 | convolution fusion | flops 1144995840 | bytes 12585984 | tf_op jit(solution)/shard_map/mlc,mn->lnc/dot_general | solution.py:93
  241.2 6.9 %copy.32 = bf16[8,1440,128]{2,0,1:T(8,128)(2,1)S(1)} copy(bf16[8,1440,128]{2,1,0:T(8,128)(2,1)S(1)} %fusion.14) | data formatting | bytes 5898240 | tf_op jit(solution)/shard_map/convert_element_type | solution.py:96
  248.0 38.6 %all_to_all.46 = bf16[8,1440,128]{2,0,1:T(8,128)(2,1)S(1)} all-to-all(bf16[8,1440,128]{2,0,1:T(8,128)(2,1)S(1)} %copy.32), channel_id=1, replica_groups=mesh['lat'=64,'ch'=4] {'ch'}, dimensions={1} | all-to-all | bytes 5898240 | tf_op jit(solution)/shard_map/all_to_all | solution.py:97
  286.6 1.6 copy-done.1
  288.2 0.4 convert.25
  288.6 8.1 %bitcast_reduce_fusion = f32[8,360]{1,0:T(8,128)S(1)} fusion(f32[8,4,360,128]{3,0,2,1:T(8,128)S(1)} %convert.25), kind=kLoop, calls=%fused_computation.15 | loop fusion | flops 1471680 | bytes 5909760 | tf_op jit(solution)/shard_map/reduce_sum | solution.py:33
  296.7 41.6 %fusion.13 = f32[8,360]{1,0:T(8,128)S(1)} fusion(f32[8,360]{1,0:T(8,128)S(1)} %broadcast_multiply_fusion, f32[8,4,360,128]{3,0,2,1:T(8,128)S(1)} %convert.25), kind=kLoop, calls=%fused_computation.18 | loop fusion | flops 4420800 | bytes 5921280 | tf_op jit(solution)/shard_map/reduce_sum | solution.py:34
  338.4 0.1 div.17
  338.5 0.0 copy-start.10
  338.5 0.0 copy-start.11
  338.5 0.0 copy-start.13
  338.5 6.7 %copy.33 = f32[8,4,360,128]{3,1,2,0:T(4,128)} copy(bf16[8,4,360,128]{3,0,2,1:T(8,128)(2,1)} %bitcast.131) | data formatting | bytes 8847360 | tf_op jit(solution)/shard_map/convert_element_type | solution.py:32
  345.2 0.1 rsqrt.12
  345.3 0.0 copy-done
  345.4 14.0 %fusion.11 = bf16[2880,512]{1,0:T(8,128)(2,1)} fusion(f32[360,8,4,128]{3,2,1,0:T(4,128)} %bitcast.134, bf16[1024,512]{1,0:T(8,128)(2,1)S(1)} %copy-done, f32[1024]{0:T(1024)S(1)} %copy-done.11, bf16[512,1024]{1,0:T(8,128)(2,1)S(1)} %copy-done.10, f32[512]{0:T(512)S(1)} %copy-done.13, f32[2880]{0:T(1024)S(1)} %rsqrt.12, f32[2880]{0:T(1024)S(1)} %div.17), kind=kOutput, calls=%fused_computation.14 | convolution fusion | flops 6078136320 | bytes 10973696 | tf_op jit(solution)/shard_map/dot_general | solution.py:38
  (19 shorter events, 0.0 us)
Async XLA Ops:
  6.5 338.8 %copy-start = (bf16[1024,512]{1,0:T(8,128)(2,1)S(1)}, bf16[1024,512]{1,0:T(8,128)(2,1)}, u32[]{:S(2)}) copy-start(bf16[1024,512]{1,0:T(8,128)(2,1)} %param.21) | copy-start | bytes 3145732
  6.5 11.5 %copy-start.5 = (s32[384]{0:T(512)S(1)}, s32[384]{0:T(512)}, u32[]{:S(2)}) copy-start(s32[384]{0:T(512)} %param.13) | copy-start | bytes 4612
  6.5 112.2 %all-gather.7.cloned.1.call-start = ((), (), s32[]{:S(2)}) async-start(), calls=%async_computation.4 | async-start | bytes 2949120 | tf_op jit(solution)/shard_map/all_gather | solution.py:77
  6.5 11.5 %copy-start.6 = (bf16[8,1440,128]{2,1,0:T(8,128)(2,1)S(1)}, bf16[8,1440,128]{2,1,0:T(8,128)(2,1)}, u32[]{:S(2)}) copy-start(bf16[8,1440,128]{2,1,0:T(8,128)(2,1)} %param.11) | copy-start | bytes 8847364
  29.3 52.0 %copy-start.8 = (bf16[6,384,512]{2,1,0:T(8,128)(2,1)S(1)}, bf16[6,384,512]{2,1,0:T(8,128)(2,1)}, u32[]{:S(2)}) copy-start(bf16[6,384,512]{2,1,0:T(8,128)(2,1)} %param.12) | copy-start | bytes 7077892
  29.3 52.0 %copy-start.12 = (f32[512]{0:T(512)S(1)}, f32[512]{0:T(512)}, u32[]{:S(2)}) copy-start(f32[512]{0:T(512)} %param.14) | copy-start | bytes 6148
  83.2 77.6 %all-gather.5.cloned.1.call-start = ((), (), s32[]{:S(2)}) async-start(), calls=%async_computation.3 | async-start | bytes 2949120 | tf_op jit(solution)/shard_map/all_gather | solution.py:76
  118.7 2.6 copy-start.3
  160.8 2.7 copy-start.2
  160.8 2.7 copy-start.4
  163.4 1.9 copy-start.9
  169.3 50.8 %all-to-all-start.1 = ((bf16[6,512,2,128]{3,2,0,1:T(2,128)(2,1)}), bf16[6,512,2,128]{3,2,0,1:T(2,128)(2,1)S(1)}, u32[]{:S(2)}, u32[]{:S(2)}) async-start(bf16[6,512,2,128]{3,2,0,1:T(2,128)(2,1)} %copy.27), calls=%async_computation.1 | async-start | bytes 3145728 | tf_op jit(solution)/shard_map/all_to_all | solution.py:91
  220.7 9.6 %copy-start.7 = (bf16[8,1440,128]{2,1,0:T(8,128)(2,1)S(1)}, bf16[8,1440,128]{2,1,0:T(8,128)(2,1)}, u32[]{:S(2)}) copy-start(bf16[8,1440,128]{2,1,0:T(8,128)(2,1)} %param.11) | copy-start | bytes 8847364
  286.6 1.6 copy-start.1
  338.5 6.9 %copy-start.10 = (bf16[512,1024]{1,0:T(8,128)(2,1)S(1)}, bf16[512,1024]{1,0:T(8,128)(2,1)}, u32[]{:S(2)}) copy-start(bf16[512,1024]{1,0:T(8,128)(2,1)} %param.19) | copy-start | bytes 3145732
  338.5 6.9 %copy-start.11 = (f32[1024]{0:T(1024)S(1)}, f32[1024]{0:T(1024)}, u32[]{:S(2)}) copy-start(f32[1024]{0:T(1024)} %param.20) | copy-start | bytes 12292
  338.5 6.9 %copy-start.13 = (f32[512]{0:T(512)S(1)}, f32[512]{0:T(512)}, u32[]{:S(2)}) copy-start(f32[512]{0:T(512)} %param.18) | copy-start | bytes 6148
Sparse Core Ops, SparseCore 0:
  83.3 35.3 all-gather.6
  120.5 40.2 all-gather.4
where the time goes:
time: 374 us; the launch traced here: 366 us
  waiting for transfers between devices  112 us (30%)
  blocking collectives  90.5 us (24%)
  matrix products  66.6 us (18%)
  other arithmetic  50.3 us (13%)
  local copies, waits for them, and re-layouts  22.7 us (6%)
  between operations  13.9 us (4%)
  starting transfers between devices  10.9 us (3%)
    all_to_all x1, blocking collectives, body(): lax.all_to_all(spectra, 'lat', split_axis=0, concat_axis=1, tiled=True)  52 us
    reduce_sum x1, other arithmetic, point_layer(): spread = jnp.mean((values - center) ** 2, axis=-1, keepdims=True)  41.6 us
    all_to_all x1, waiting for transfers between devices, body(): block = lax.all_to_all(back, 'lat', split_axis=1, concat_axis=0, tiled=True)  39.9 us
    all_to_all x1, blocking collectives, body(): lax.all_to_all(summed, 'ch', split_axis=1, concat_axis=2, tiled=True)  38.6 us
    all_gather x1, waiting for transfers between devices, body(): lax.all_gather(coef_re, 'ch', axis=2, tiled=True)  37.8 us
    all_gather x1, waiting for transfers between devices, body(): lax.all_gather(coef_im, 'ch', axis=2, tiled=True)  33.2 us
    dot_general x1, matrix products, point_layer(): jnp.dot(hidden, mlp_out, preferred_element_type=jnp.float32)  14 us
    dot_general x1, matrix products, body(): jnp.einsum('lnc,nm->mlc', grid, fwd_sin, preferred_element_type=jnp.float32)  11.4 us
  transfers between devices with their start and end apart: 3, of which 3 were waited for; matrix products, arithmetic and copies ran while one was open for 2% of the time, Pallas kernels for 0%

commit v1 on v0

v1 whole, which is shorter than its diff:
```python
import math

import jax
import jax.numpy as jnp
import numpy as np
import ml_dtypes
from jax import lax
from jax.experimental import pallas as pl
from jax.experimental.pallas import tpu as pltpu
from jax.sharding import PartitionSpec as P

NLON = 1440
MODES = 384
NL = 64
NX = 4
CYC = 8
ROWS = 6
CB = 128
LB = MODES // NX
LON = NLON // NX
KP = ROWS // 2
MESH = pl.DeviceIdType.MESH
BF = jnp.bfloat16
F32 = jnp.float32


def twiddles():
    index = np.arange(MODES)[:, None] * np.arange(NLON)[None, :] % NLON
    angle = index * (2.0 * math.pi / NLON)
    table = np.stack([np.cos(angle), -np.sin(angle)]) / math.sqrt(NLON)
    return table.astype(np.float32).astype(ml_dtypes.bfloat16)


def dot(a, b):
    return jnp.dot(a, b, preferred_element_type=F32)


def kernel(
    mcol,
    mrow,
    quad,
    lng,
    bias,
    grid_h,
    tw_h,
    twt_h,
    leg_h,
    mr_h,
    mi_h,
    gain_h,
    win_h,
    wout_h,
    out_h,
    grid_v,
    tw_v,
    twt_v,
    leg_v,
    legt,
    mr_v,
    mi_v,
    gain_v,
    win_v,
    wout_v,
    stage,
    sbuf,
    rbuf,
    cs,
    cr,
    wm,
    fs,
    fr,
    es,
    er,
    itab,
    xst,
    gs,
    gr,
    ov,
    load_sem,
    s_snd,
    s_rcv,
    c_snd,
    c_rcv,
    f_snd,
    f_rcv,
    e_snd,
    e_rcv,
    g_snd,
    g_rcv,
    o_sem,
):
    me = lax.axis_index("lat")
    x = lax.axis_index("ch")

    loads = [
        pltpu.make_async_copy(src, dst, load_sem.at[i])
        for i, (src, dst) in enumerate(
            [
                (tw_h, tw_v),
                (grid_h, grid_v),
                (leg_h, leg_v),
                (mr_h, mr_v),
                (mi_h, mi_v),
                (twt_h, twt_v),
                (gain_h.at[pl.ds(pl.multiple_of(x * LB, LB), LB)], gain_v),
                (win_h, win_v),
                (wout_h, wout_v),
            ]
        )
    ]
    for load in loads:
        load.start()

    barrier = pltpu.get_barrier_semaphore()

    @pl.loop(1, NL)
    def _(s):
        pl.semaphore_signal(
            barrier, inc=1, device_id=(lax.rem(me + s, NL), x), device_id_type=MESH
        )

    for s in range(1, NX):
        pl.semaphore_signal(
            barrier, inc=1, device_id=(me, lax.rem(x + s, NX)), device_id_type=MESH
        )

    def lat_send(src, dst, snd, rcv):
        @pl.loop(1, NL)
        def _(s):
            j = lax.rem(me + s, NL)
            pltpu.make_async_remote_copy(
                src_ref=src.at[j],
                dst_ref=dst.at[me],
                send_sem=snd,
                recv_sem=rcv,
                device_id=(j, x),
                device_id_type=MESH,
            ).start()

        pltpu.make_async_copy(src.at[me], dst.at[me], rcv).start()

    def ch_send(src, dst, snd, rcv):
        for s in (2, 1, 3):
            i = lax.rem(x + s, NX)
            pltpu.make_async_remote_copy(
                src_ref=src.at[i],
                dst_ref=dst.at[x],
                send_sem=snd,
                recv_sem=rcv,
                device_id=(me, i),
                device_id_type=MESH,
            ).start()
        pltpu.make_async_copy(src.at[x], dst.at[x], rcv).start()

    def take(ref, sem):
        pltpu.make_async_copy(ref, ref, sem).wait()

    loads[0].wait()
    loads[1].wait()
    lane = lax.broadcasted_iota(jnp.int32, (2 * NL, MODES), 1)
    for kp in range(KP):
        hot = jnp.where(mcol[kp * 2 * NL : (kp + 1) * 2 * NL, :] == lane, 1.0, 0.0).astype(BF)
        table = jnp.concatenate(
            [dot(hot, tw_v[0]).astype(BF), dot(hot, tw_v[1]).astype(BF)], axis=0
        )
        for p in range(CYC // 2):
            res = dot(table, jnp.concatenate([grid_v[2 * p], grid_v[2 * p + 1]], axis=1))
            for reim in range(2):
                for k2 in range(2):
                    at = (reim * 2 + k2) * NL
                    for c in range(2):
                        row = k2 * 16 + reim * 8 + 2 * p + c
                        stage[pl.ds(row, NL, stride=32), :] = res[
                            at : at + NL, c * CB : (c + 1) * CB
                        ]
        sbuf[kp] = stage[...].astype(BF).reshape(NL, 32, CB)
        if kp == 0:
            pl.semaphore_wait(barrier, NL - 1 + NX - 1)
        lat_send(sbuf.at[kp], rbuf.at[kp], s_snd.at[kp], s_rcv.at[kp])

    loads[2].wait()
    for k in range(ROWS):
        values = leg_v[k]
        legt[k] = values.T
        leg_v[k] = (values.astype(F32) * quad[...]).astype(BF)
    loads[3].wait()
    loads[4].wait()
    for xs in range(NX):
        for xd in range(NX):
            re = mr_v[xs * CB : (xs + 1) * CB, xd * CB : (xd + 1) * CB]
            im = mi_v[xs * CB : (xs + 1) * CB, xd * CB : (xd + 1) * CB]
            r0, c0 = xs * 2 * CB, xd * 2 * CB
            wm[r0 : r0 + CB, c0 : c0 + CB] = re
            wm[r0 : r0 + CB, c0 + CB : c0 + 2 * CB] = im
            wm[r0 + CB : r0 + 2 * CB, c0 : c0 + CB] = -im
            wm[r0 + CB : r0 + 2 * CB, c0 + CB : c0 + 2 * CB] = re
    loads[5].wait()
    order = lax.broadcasted_iota(jnp.int32, (MODES, MODES), 0)
    scale = jnp.where(order == 0, 1.0, 2.0)
    hot = jnp.where(mrow[...] == order, scale, 0.0).astype(BF)
    for reim in range(2):
        itab[:, reim * MODES : (reim + 1) * MODES] = dot(twt_v[reim], hot).astype(BF)
    loads[6].wait()

    upper = lax.broadcasted_iota(jnp.int32, (NL, 8, CB), 1) < 4

    def analyse(kp):
        take(rbuf.at[kp], s_rcv.at[kp])
        for k2 in range(2):
            got = rbuf[kp, :, k2 * 16 : (k2 + 1) * 16, :].astype(F32)
            spec = jnp.concatenate(
                [
                    got[:, :8, :].reshape(NL * 8, CB).astype(BF),
                    got[:, 8:, :].reshape(NL * 8, CB).astype(BF),
                ],
                axis=1,
            )
            coef = dot(leg_v[2 * kp + k2], spec).astype(BF)
            for i in range(NX):
                cs[kp, i, k2] = coef[i * LB : (i + 1) * LB]
        ch_send(cs.at[kp], cr.at[kp], c_snd.at[kp], c_rcv.at[kp])

    def mix(kp):
        take(cr.at[kp], c_rcv.at[kp])
        lhs = jnp.concatenate([cr[kp, i].reshape(2 * LB, 2 * CB) for i in range(NX)], axis=1)
        res = dot(lhs, wm[...])
        for i in range(NX):
            part = gain_v[:, i * CB : (i + 1) * CB]
            part = jnp.concatenate([part, part], axis=1)
            part = jnp.concatenate([part, part], axis=0)
            filt = (res[:, i * 2 * CB : (i + 1) * 2 * CB] * part).astype(BF)
            fs[kp, i] = filt.reshape(2, LB, 2 * CB)
        ch_send(fs.at[kp], fr.at[kp], f_snd.at[kp], f_rcv.at[kp])

    def synthesise(kp):
        take(fr.at[kp], f_rcv.at[kp])
        halves = [[], []]
        for k2 in range(2):
            filt = jnp.concatenate([fr[kp, i, k2] for i in range(NX)], axis=0)
            back = dot(legt[2 * kp + k2], filt)
            re = back[:, :CB].reshape(NL, 8, CB)
            im = back[:, CB:].reshape(NL, 8, CB)
            halves[0].append(jnp.where(upper, re, pltpu.roll(im, 4, 1)))
            halves[1].append(jnp.where(upper, pltpu.roll(re, 4, 1), im))
        for h in range(2):
            es[h, kp] = jnp.concatenate(halves[h], axis=1).astype(BF)

    def back_send(h, kp):
        lat_send(es.at[h, kp], er.at[h, kp], e_snd.at[h, kp], e_rcv.at[h, kp])

    def waves(h):
        for kp in range(KP):
            take(er.at[h, kp], e_rcv.at[h, kp])
        xst[...] = er[h].astype(F32).reshape(KP * NL * 16, CB)
        for q in range(2):
            p = 2 * h + q
            cols = []
            for c in range(2):
                cols.append(
                    jnp.concatenate(
                        [
                            xst[
                                pl.ds(kp * NL * 16 + k2 * 8 + reim * 4 + 2 * q + c, NL, stride=16),
                                :,
                            ]
                            for reim in range(2)
                            for kp in range(KP)
                            for k2 in range(2)
                        ],
                        axis=0,
                    ).astype(BF)
                )
            wave = dot(itab[...], jnp.concatenate(cols, axis=1))
            both = [grid_v[2 * p + c].astype(F32) + wave[:, c * CB : (c + 1) * CB] for c in range(2)]
            for i in range(NX):
                gs[p, i] = jnp.concatenate(
                    [b[i * LON : (i + 1) * LON] for b in both], axis=0
                ).astype(BF)
            ch_send(gs.at[p], gr.at[p], g_snd.at[p], g_rcv.at[p])

    step = 240

    def points(p):
        take(gr.at[p], g_rcv.at[p])

        @pl.loop(0, 2 * LON // step)
        def _(t):
            at = pl.ds(pl.multiple_of(t * step, 16), step)
            values = jnp.concatenate([gr[p, i, at, :] for i in range(NX)], axis=1).astype(F32)
            center = jnp.mean(values, axis=-1, keepdims=True)
            moved = values - center
            spread = jnp.mean(moved * moved, axis=-1, keepdims=True)
            normed = (moved * lax.rsqrt(spread + 1e-05) * lng[...]).astype(BF)
            inner = dot(normed, win_v[...]) + bias[...]
            hidden = jax.nn.gelu(inner, approximate=True).astype(BF)
            ov[p, at, :] = (values + dot(hidden, wout_v[...])).astype(BF)

        pltpu.make_async_copy(ov.at[p], out_h.at[p], o_sem.at[p]).start()

    for kp in range(KP):
        analyse(kp)
        mix(kp)
        synthesise(kp)
        back_send(0, kp)
    for kp in range(KP):
        back_send(1, kp)
    waves(0)
    loads[7].wait()
    loads[8].wait()
    points(0)
    points(1)
    waves(1)
    points(2)
    points(3)

    for kp in range(KP):
        take(sbuf.at[kp, pl.ds(0, NL - 1)], s_snd.at[kp])
        take(cs.at[kp, pl.ds(0, NX - 1)], c_snd.at[kp])
        take(fs.at[kp, pl.ds(0, NX - 1)], f_snd.at[kp])
        for h in range(2):
            take(es.at[h, kp, pl.ds(0, NL - 1)], e_snd.at[h, kp])
    for p in range(CYC // 2):
        take(gs.at[p, pl.ds(0, NX - 1)], g_snd.at[p])
        pltpu.make_async_copy(ov.at[p], out_h.at[p], o_sem.at[p]).wait()


def body(
    grid,
    legendre,
    m_order,
    quad_weights,
    mix_real,
    mix_imag,
    spec_gain,
    ln_gain,
    mlp_in,
    mlp_bias,
    mlp_out,
):
    table = twiddles()
    order = m_order.reshape(NL, ROWS).T.reshape(MODES)
    vm = pl.BlockSpec(memory_space=pltpu.VMEM)
    hbm = pl.BlockSpec(memory_space=pl.ANY)
    dma = pltpu.SemaphoreType.DMA
    out = pl.pallas_call(
        kernel,
        out_shape=jax.ShapeDtypeStruct((CYC // 2, 2 * LON, NX * CB), BF),
        in_specs=[vm] * 5 + [hbm] * 9,
        out_specs=hbm,
        scratch_shapes=[
            pltpu.VMEM((CYC, NLON, CB), BF),
            pltpu.VMEM((2, MODES, NLON), BF),
            pltpu.VMEM((2, NLON, MODES), BF),
            pltpu.VMEM((ROWS, MODES, NL * CYC), BF),
            pltpu.VMEM((ROWS, NL * CYC, MODES), BF),
            pltpu.VMEM(mix_real.shape, BF),
            pltpu.VMEM(mix_imag.shape, BF),
            pltpu.VMEM((LB, NX * CB), F32),
            pltpu.VMEM(mlp_in.shape, BF),
            pltpu.VMEM(mlp_out.shape, BF),
            pltpu.VMEM((NL * 32, CB), F32),
            pltpu.VMEM((KP, NL, 32, CB), BF),
            pltpu.VMEM((KP, NL, 32, CB), BF),
            pltpu.VMEM((KP, NX, 2, LB, 2 * CB), BF),
            pltpu.VMEM((KP, NX, 2, LB, 2 * CB), BF),
            pltpu.VMEM((2 * NX * CB, 2 * NX * CB), BF),
            pltpu.VMEM((KP, NX, 2, LB, 2 * CB), BF),
            pltpu.VMEM((KP, NX, 2, LB, 2 * CB), BF),
            pltpu.VMEM((2, KP, NL, 16, CB), BF),
            pltpu.VMEM((2, KP, NL, 16, CB), BF),
            pltpu.VMEM((NLON, 2 * MODES), BF),
            pltpu.VMEM((KP * NL * 16, CB), F32),
            pltpu.VMEM((CYC // 2, NX, 2 * LON, CB), BF),
            pltpu.VMEM((CYC // 2, NX, 2 * LON, CB), BF),
            pltpu.VMEM((CYC // 2, 2 * LON, NX * CB), BF),
            dma((9,)),
            dma((KP,)),
            dma((KP,)),
            dma((KP,)),
            dma((KP,)),
            dma((KP,)),
            dma((KP,)),
            dma((2, KP)),
            dma((2, KP)),
            dma((CYC // 2,)),
            dma((CYC // 2,)),
            dma((CYC // 2,)),
        ],
        compiler_params=pltpu.CompilerParams(
            collective_id=0, has_side_effects=True, vmem_limit_bytes=60 << 20
        ),
        name="sfno_block",
    )(
        order[:, None],
        order[None, :],
        quad_weights[None, :],
        ln_gain[None, :],
        mlp_bias[None, :],
        grid,
        jnp.asarray(table),
        jnp.asarray(np.ascontiguousarray(table.transpose(0, 2, 1))),
        legendre,
        mix_real,
        mix_imag,
        spec_gain,
        mlp_in,
        mlp_out,
    )
    return out.reshape(CYC, LON, NX * CB)


def solution(mesh):
    placed = (P("lat", None, "ch"), P("lat", None, None)) + (P(),) * 9
    return jax.shard_map(
        body, mesh=mesh, in_specs=placed, out_specs=P("lat", "ch", None), check_vma=False
    )
```

time: 374 us -> 133 us (0.36)
  the two profiles are of different devices: /device:TPU:16 before, /device:TPU:1 now
where the time goes in v1:
time: 133 us
  Pallas kernels  127 us (95%)
  local copies, waits for them, and re-layouts  5.98 us (4%)
    pallas_call x1, Pallas kernels, body(): pl.pallas_call(kernel, out_shape=jax.ShapeDtypeStruct((CYC // 2, 2 * LON,...  127 us
    unnamed x1, local copies, waits for them, and re-layouts  3.62 us

profile of v1, /device:TPU:1, one launch (start us, length us, event | category | flops | bytes accessed | tf_op | source)
XLA Modules:
  0.0 133.3 jit_solution(16812504808496926758)
XLA Ops:
  0.0 0.8 reshape.6
  0.8 0.1 copy.14
  0.9 0.6 broadcast_in_dim_reshape.7.mrow
  1.5 0.8 broadcast_in_dim_reshape.8.mcol
  2.4 127.3 %sfno_block.1 = bf16[4,720,512]{2,1,0:T(8,128)(2,1)} custom-call(s32[384,1]{1,0:T(8,128)} %broadcast_in_dim_reshape.8.mcol, s32[1,384]{1,0:T(1,128)} %broadcast_in_dim_reshape.7.mrow, f32[1,512]{1,0:T(1,128)} %bitcast.8, f32[1,512]{1,0:T(1,128)} %bitcast.9, f32[1,1024]{1,0:T(1,128)} %bitcast.7, bf16[8,1440,128]{2,1,0:T(8,128)(2,1)} %grid_h.1, ...), custom_call_target="tpu_custom_call" | custom-call | tf_op jit(solution)/shard_map/sfno_block/pallas_call | solution.py:345
  129.7 3.6 %copy.18 = bf16[8,360,512]{2,1,0:T(8,128)(2,1)} copy(bf16[8,360,512]{2,1,0:T(8,128)(2,1)} %bitcast.5) | data formatting | bytes 5898240

commit v2 on v1

--- a/solution.py
+++ b/solution.py
@@ -19,6 +19,7 @@
 LB = MODES // NX
 LON = NLON // NX
 KP = ROWS // 2
+PIECES = [(0, 0, 720), (1, 0, 720), (2, 0, 720), (3, 0, 368), (3, 368, 352)]
 MESH = pl.DeviceIdType.MESH
 BF = jnp.bfloat16
 F32 = jnp.float32
@@ -36,8 +37,7 @@
 
 
 def kernel(
-    mcol,
-    mrow,
+    morder,
     quad,
     lng,
     bias,
@@ -155,13 +155,18 @@
     def take(ref, sem):
         pltpu.make_async_copy(ref, ref, sem).wait()
 
+    order = lax.broadcasted_iota(jnp.int32, (MODES, MODES), 0)
+    place = lax.broadcasted_iota(jnp.int32, (MODES, MODES), 1)
+    moved = jnp.where(order == ROWS * (place % NL) + place // NL, 1.0, 0.0).astype(BF)
+    hot = dot(jnp.where(morder[...] == order, 1.0, 0.0).astype(BF), moved)
+    pick = hot.T.astype(BF)
+
     loads[0].wait()
     loads[1].wait()
-    lane = lax.broadcasted_iota(jnp.int32, (2 * NL, MODES), 1)
     for kp in range(KP):
-        hot = jnp.where(mcol[kp * 2 * NL : (kp + 1) * 2 * NL, :] == lane, 1.0, 0.0).astype(BF)
+        rows = pick[kp * 2 * NL : (kp + 1) * 2 * NL]
         table = jnp.concatenate(
-            [dot(hot, tw_v[0]).astype(BF), dot(hot, tw_v[1]).astype(BF)], axis=0
+            [dot(rows, tw_v[0]).astype(BF), dot(rows, tw_v[1]).astype(BF)], axis=0
         )
         for p in range(CYC // 2):
             res = dot(table, jnp.concatenate([grid_v[2 * p], grid_v[2 * p + 1]], axis=1))
@@ -169,14 +174,17 @@
                 for k2 in range(2):
                     at = (reim * 2 + k2) * NL
                     for c in range(2):
-                        row = k2 * 16 + reim * 8 + 2 * p + c
-                        stage[pl.ds(row, NL, stride=32), :] = res[
+                        row = k2 * NL * 16 + reim * 8 + 2 * p + c
+                        stage[pl.ds(row, NL, stride=16), :] = res[
                             at : at + NL, c * CB : (c + 1) * CB
                         ]
-        sbuf[kp] = stage[...].astype(BF).reshape(NL, 32, CB)
+        for k2 in range(2):
+            part = stage[k2 * NL * 16 : (k2 + 1) * NL * 16]
+            sbuf[2 * kp + k2] = part.astype(BF).reshape(NL, 16, CB)
         if kp == 0:
             pl.semaphore_wait(barrier, NL - 1 + NX - 1)
-        lat_send(sbuf.at[kp], rbuf.at[kp], s_snd.at[kp], s_rcv.at[kp])
+        for k in (2 * kp, 2 * kp + 1):
+            lat_send(sbuf.at[k], rbuf.at[k], s_snd.at[k], s_rcv.at[k])
 
     loads[2].wait()
     for k in range(ROWS):
@@ -195,55 +203,47 @@
             wm[r0 + CB : r0 + 2 * CB, c0 : c0 + CB] = -im
             wm[r0 + CB : r0 + 2 * CB, c0 + CB : c0 + 2 * CB] = re
     loads[5].wait()
-    order = lax.broadcasted_iota(jnp.int32, (MODES, MODES), 0)
-    scale = jnp.where(order == 0, 1.0, 2.0)
-    hot = jnp.where(mrow[...] == order, scale, 0.0).astype(BF)
+    hot = (hot * jnp.where(order == 0, 1.0, 2.0)).astype(BF)
     for reim in range(2):
         itab[:, reim * MODES : (reim + 1) * MODES] = dot(twt_v[reim], hot).astype(BF)
     loads[6].wait()
 
     upper = lax.broadcasted_iota(jnp.int32, (NL, 8, CB), 1) < 4
 
-    def analyse(kp):
-        take(rbuf.at[kp], s_rcv.at[kp])
-        for k2 in range(2):
-            got = rbuf[kp, :, k2 * 16 : (k2 + 1) * 16, :].astype(F32)
-            spec = jnp.concatenate(
-                [
-                    got[:, :8, :].reshape(NL * 8, CB).astype(BF),
-                    got[:, 8:, :].reshape(NL * 8, CB).astype(BF),
-                ],
-                axis=1,
-            )
-            coef = dot(leg_v[2 * kp + k2], spec).astype(BF)
-            for i in range(NX):
-                cs[kp, i, k2] = coef[i * LB : (i + 1) * LB]
-        ch_send(cs.at[kp], cr.at[kp], c_snd.at[kp], c_rcv.at[kp])
-
-    def mix(kp):
-        take(cr.at[kp], c_rcv.at[kp])
-        lhs = jnp.concatenate([cr[kp, i].reshape(2 * LB, 2 * CB) for i in range(NX)], axis=1)
-        res = dot(lhs, wm[...])
+    def analyse(k):
+        got = rbuf[k].astype(F32)
+        spec = jnp.concatenate(
+            [
+                got[:, :8, :].reshape(NL * 8, CB).astype(BF),
+                got[:, 8:, :].reshape(NL * 8, CB).astype(BF),
+            ],
+            axis=1,
+        )
+        cs[k] = dot(leg_v[k], spec).astype(BF).reshape(NX, LB, 2 * CB)
+        ch_send(cs.at[k], cr.at[k], c_snd.at[k], c_rcv.at[k])
+
+    def mix(k):
+        take(cr.at[k], c_rcv.at[k])
+        res = dot(jnp.concatenate([cr[k, i] for i in range(NX)], axis=1), wm[...])
         for i in range(NX):
             part = gain_v[:, i * CB : (i + 1) * CB]
             part = jnp.concatenate([part, part], axis=1)
-            part = jnp.concatenate([part, part], axis=0)
-            filt = (res[:, i * 2 * CB : (i + 1) * 2 * CB] * part).astype(BF)
-            fs[kp, i] = filt.reshape(2, LB, 2 * CB)
-        ch_send(fs.at[kp], fr.at[kp], f_snd.at[kp], f_rcv.at[kp])
-
-    def synthesise(kp):
-        take(fr.at[kp], f_rcv.at[kp])
-        halves = [[], []]
-        for k2 in range(2):
-            filt = jnp.concatenate([fr[kp, i, k2] for i in range(NX)], axis=0)
-            back = dot(legt[2 * kp + k2], filt)
-            re = back[:, :CB].reshape(NL, 8, CB)
-            im = back[:, CB:].reshape(NL, 8, CB)
-            halves[0].append(jnp.where(upper, re, pltpu.roll(im, 4, 1)))
-            halves[1].append(jnp.where(upper, pltpu.roll(re, 4, 1), im))
+            fs[k, i] = (res[:, i * 2 * CB : (i + 1) * 2 * CB] * part).astype(BF)
+        ch_send(fs.at[k], fr.at[k], f_snd.at[k], f_rcv.at[k])
+
+    def synthesise(k):
+        take(fr.at[k], f_rcv.at[k])
+        back = dot(legt[k], fr[k].reshape(MODES, 2 * CB))
+        re = back[:, :CB].reshape(NL, 8, CB)
+        im = back[:, CB:].reshape(NL, 8, CB)
+        return (
+            jnp.where(upper, re, pltpu.roll(im, 4, 1)),
+            jnp.where(upper, pltpu.roll(re, 4, 1), im),
+        )
+
+    def pack(kp, first, second):
         for h in range(2):
-            es[h, kp] = jnp.concatenate(halves[h], axis=1).astype(BF)
+            es[h, kp] = jnp.concatenate([first[h], second[h]], axis=1).astype(BF)
 
     def back_send(h, kp):
         lat_send(es.at[h, kp], er.at[h, kp], e_snd.at[h, kp], e_rcv.at[h, kp])
@@ -276,52 +276,62 @@
                 gs[p, i] = jnp.concatenate(
                     [b[i * LON : (i + 1) * LON] for b in both], axis=0
                 ).astype(BF)
-            ch_send(gs.at[p], gr.at[p], g_snd.at[p], g_rcv.at[p])
-
-    step = 240
-
-    def points(p):
-        take(gr.at[p], g_rcv.at[p])
-
-        @pl.loop(0, 2 * LON // step)
-        def _(t):
-            at = pl.ds(pl.multiple_of(t * step, 16), step)
-            values = jnp.concatenate([gr[p, i, at, :] for i in range(NX)], axis=1).astype(F32)
-            center = jnp.mean(values, axis=-1, keepdims=True)
-            moved = values - center
-            spread = jnp.mean(moved * moved, axis=-1, keepdims=True)
-            normed = (moved * lax.rsqrt(spread + 1e-05) * lng[...]).astype(BF)
-            inner = dot(normed, win_v[...]) + bias[...]
-            hidden = jax.nn.gelu(inner, approximate=True).astype(BF)
-            ov[p, at, :] = (values + dot(hidden, wout_v[...])).astype(BF)
-
-        pltpu.make_async_copy(ov.at[p], out_h.at[p], o_sem.at[p]).start()
+            for t, (pair, at, n) in enumerate(PIECES):
+                if pair == p:
+                    part = pl.ds(at, n)
+                    ch_send(
+                        gs.at[p, :, part], gr.at[p, :, part], g_snd.at[t], g_rcv.at[t]
+                    )
+
+    def points(t):
+        p, at, n = PIECES[t]
+        part = pl.ds(at, n)
+        take(gr.at[p, :, part], g_rcv.at[t])
+        values = jnp.concatenate([gr[p, i, part, :] for i in range(NX)], axis=1).astype(F32)
+        center = jnp.mean(values, axis=-1, keepdims=True)
+        moved = values - center
+        spread = jnp.mean(moved * moved, axis=-1, keepdims=True)
+        normed = (moved * lax.rsqrt(spread + 1e-05) * lng[...]).astype(BF)
+        inner = dot(normed, win_v[...]) + bias[...]
+        hidden = jax.nn.gelu(inner, approximate=True).astype(BF)
+        ov[p, part, :] = (values + dot(hidden, wout_v[...])).astype(BF)
+        pltpu.make_async_copy(ov.at[p, part], out_h.at[p, part], o_sem.at[t]).start()
 
     for kp in range(KP):
-        analyse(kp)
-        mix(kp)
-        synthesise(kp)
-        back_send(0, kp)
+        a, b = 2 * kp, 2 * kp + 1
+        take(rbuf.at[a], s_rcv.at[a])
+        analyse(a)
+        mix(a)
+        take(rbuf.at[b], s_rcv.at[b])
+        analyse(b)
+        if kp == KP - 1:
+            back_send(0, 0)
+            back_send(0, 1)
+        first = synthesise(a)
+        mix(b)
+        pack(kp, first, synthesise(b))
+    back_send(0, KP - 1)
     for kp in range(KP):
         back_send(1, kp)
-    waves(0)
     loads[7].wait()
     loads[8].wait()
+    waves(0)
     points(0)
-    points(1)
     waves(1)
-    points(2)
-    points(3)
-
+    for t in range(1, len(PIECES)):
+        points(t)
+
+    for k in range(ROWS):
+        take(sbuf.at[k, pl.ds(0, NL - 1)], s_snd.at[k])
+        take(cs.at[k, pl.ds(0, NX - 1)], c_snd.at[k])
+        take(fs.at[k, pl.ds(0, NX - 1)], f_snd.at[k])
     for kp in range(KP):
-        take(sbuf.at[kp, pl.ds(0, NL - 1)], s_snd.at[kp])
-        take(cs.at[kp, pl.ds(0, NX - 1)], c_snd.at[kp])
-        take(fs.at[kp, pl.ds(0, NX - 1)], f_snd.at[kp])
         for h in range(2):
             take(es.at[h, kp, pl.ds(0, NL - 1)], e_snd.at[h, kp])
-    for p in range(CYC // 2):
-        take(gs.at[p, pl.ds(0, NX - 1)], g_snd.at[p])
-        pltpu.make_async_copy(ov.at[p], out_h.at[p], o_sem.at[p]).wait()
+    for t, (p, at, n) in enumerate(PIECES):
+        part = pl.ds(at, n)
+        take(gs.at[p, pl.ds(0, NX - 1), part], g_snd.at[t])
+        pltpu.make_async_copy(ov.at[p, part], out_h.at[p, part], o_sem.at[t]).wait()
 
 
 def body(
@@ -338,14 +348,13 @@
     mlp_out,
 ):
     table = twiddles()
-    order = m_order.reshape(NL, ROWS).T.reshape(MODES)
     vm = pl.BlockSpec(memory_space=pltpu.VMEM)
     hbm = pl.BlockSpec(memory_space=pl.ANY)
     dma = pltpu.SemaphoreType.DMA
     out = pl.pallas_call(
         kernel,
         out_shape=jax.ShapeDtypeStruct((CYC // 2, 2 * LON, NX * CB), BF),
-        in_specs=[vm] * 5 + [hbm] * 9,
+        in_specs=[vm] * 4 + [hbm] * 9,
         out_specs=hbm,
         scratch_shapes=[
             pltpu.VMEM((CYC, NLON, CB), BF),
@@ -359,13 +368,13 @@
             pltpu.VMEM(mlp_in.shape, BF),
             pltpu.VMEM(mlp_out.shape, BF),
             pltpu.VMEM((NL * 32, CB), F32),
-            pltpu.VMEM((KP, NL, 32, CB), BF),
-            pltpu.VMEM((KP, NL, 32, CB), BF),
-            pltpu.VMEM((KP, NX, 2, LB, 2 * CB), BF),
-            pltpu.VMEM((KP, NX, 2, LB, 2 * CB), BF),
+            pltpu.VMEM((ROWS, NL, 16, CB), BF),
+            pltpu.VMEM((ROWS, NL, 16, CB), BF),
+            pltpu.VMEM((ROWS, NX, LB, 2 * CB), BF),
+            pltpu.VMEM((ROWS, NX, LB, 2 * CB), BF),
             pltpu.VMEM((2 * NX * CB, 2 * NX * CB), BF),
-            pltpu.VMEM((KP, NX, 2, LB, 2 * CB), BF),
-            pltpu.VMEM((KP, NX, 2, LB, 2 * CB), BF),
+            pltpu.VMEM((ROWS, NX, LB, 2 * CB), BF),
+            pltpu.VMEM((ROWS, NX, LB, 2 * CB), BF),
             pltpu.VMEM((2, KP, NL, 16, CB), BF),
             pltpu.VMEM((2, KP, NL, 16, CB), BF),
             pltpu.VMEM((NLON, 2 * MODES), BF),
@@ -374,25 +383,24 @@
             pltpu.VMEM((CYC // 2, NX, 2 * LON, CB), BF),
             pltpu.VMEM((CYC // 2, 2 * LON, NX * CB), BF),
             dma((9,)),
-            dma((KP,)),
-            dma((KP,)),
-            dma((KP,)),
-            dma((KP,)),
-            dma((KP,)),
-            dma((KP,)),
+            dma((ROWS,)),
+            dma((ROWS,)),
+            dma((ROWS,)),
+            dma((ROWS,)),
+            dma((ROWS,)),
+            dma((ROWS,)),
             dma((2, KP)),
             dma((2, KP)),
-            dma((CYC // 2,)),
-            dma((CYC // 2,)),
-            dma((CYC // 2,)),
+            dma((len(PIECES),)),
+            dma((len(PIECES),)),
+            dma((len(PIECES),)),
         ],
         compiler_params=pltpu.CompilerParams(
             collective_id=0, has_side_effects=True, vmem_limit_bytes=60 << 20
         ),
         name="sfno_block",
     )(
-        order[:, None],
-        order[None, :],
+        m_order[None, :],
         quad_weights[None, :],
         ln_gain[None, :],
         mlp_bias[None, :],

time: 133 us -> 127 us (0.955)
  Pallas kernels: 127 us -> 122 us
    pallas_call x1, Pallas kernels: 127 us -> 122 us  [body(): pl.pallas_call(kernel, out_shape=jax.ShapeDtypeStruct((CYC // 2, 2 * LON,...]
    another operation x2 -> x0, local copies, waits for them, and re-layouts: 1.48 us -> none  [the longest x1 0.84 us: body(): order[:, None]]
where the time goes in v2:
time: 127 us
  Pallas kernels  122 us (96%)
  local copies, waits for them, and re-layouts  4.87 us (4%)
    pallas_call x1, Pallas kernels, body(): pl.pallas_call(kernel, out_shape=jax.ShapeDtypeStruct((CYC // 2, 2 * LON,...  122 us
    unnamed x1, local copies, waits for them, and re-layouts  3.62 us

profile of v2, /device:TPU:1, one launch (start us, length us, event | category | flops | bytes accessed | tf_op | source)
XLA Modules:
  0.0 126.7 jit_solution(6302145251838823407)
XLA Ops:
  0.0 1.2 broadcast_in_dim.12.morder
  1.2 121.8 %sfno_block.1 = bf16[4,720,512]{2,1,0:T(8,128)(2,1)} custom-call(s32[1,384]{1,0:T(1,128)} %broadcast_in_dim.12.morder, f32[1,512]{1,0:T(1,128)} %bitcast.6, f32[1,512]{1,0:T(1,128)} %bitcast.7, f32[1,1024]{1,0:T(1,128)} %bitcast.5, bf16[8,1440,128]{2,1,0:T(8,128)(2,1)} %grid_h.1, bf16[2,384,1440]{2,1,0:T(8,128)(2,1)} %constant.4.clone.tw_h, ...), custom_call_target="tpu_custom_call" | custom-call | tf_op jit(solution)/shard_map/sfno_block/pallas_call | solution.py:354
  123.1 3.6 %copy.15 = bf16[8,360,512]{2,1,0:T(8,128)(2,1)} copy(bf16[8,360,512]{2,1,0:T(8,128)(2,1)} %bitcast.4) | data formatting | bytes 5898240

commit v3 on v2

--- a/solution.py
+++ b/solution.py
@@ -34,6 +34,46 @@
 
 def dot(a, b):
     return jnp.dot(a, b, preferred_element_type=F32)
+
+
+def point_layer(rows, lng, win, bias, wout):
+    values = rows.astype(F32)
+    center = jnp.mean(values, axis=-1, keepdims=True)
+    moved = values - center
+    spread = jnp.mean(moved * moved, axis=-1, keepdims=True)
+    normed = (moved * lax.rsqrt(spread + 1e-05) * lng[...]).astype(BF)
+    inner = dot(normed, win[...]) + bias[...]
+    hidden = jax.nn.gelu(inner, approximate=True).astype(BF)
+    return (values + dot(hidden, wout[...])).astype(BF)
+
+
+def finish(lng, bias, win_h, wout_h, last_h, part_h, out_h, win, wout, last, hold, l_sem, i_sem, o_sem):
+    p, at, n = PIECES[-1]
+    loads = [
+        pltpu.make_async_copy(src, dst, l_sem.at[i])
+        for i, (src, dst) in enumerate([(last_h, last), (win_h, win), (wout_h, wout)])
+    ]
+    for load in loads:
+        load.start()
+
+    def move(t, src, dst, sem):
+        pair, first, rows = PIECES[t]
+        part = pl.ds(first, rows)
+        return pltpu.make_async_copy(src.at[pair, part], dst.at[pair, part], sem.at[t])
+
+    others = range(len(PIECES) - 1)
+    for t in others:
+        move(t, part_h, hold, i_sem).start()
+    for t in others:
+        move(t, part_h, hold, i_sem).wait()
+        move(t, hold, out_h, o_sem).start()
+    for load in loads:
+        load.wait()
+    rows = jnp.concatenate([last[i] for i in range(NX)], axis=1)
+    hold[p, at : at + n, :] = point_layer(rows, lng, win, bias, wout)
+    move(len(PIECES) - 1, hold, out_h, o_sem).start()
+    for t in range(len(PIECES)):
+        move(t, hold, out_h, o_sem).wait()
 
 
 def kernel(
@@ -51,6 +91,7 @@
     win_h,
     wout_h,
     out_h,
+    last_h,
     grid_v,
     tw_v,
     twt_v,
@@ -69,8 +110,10 @@
     wm,
     fs,
     fr,
-    es,
-    er,
+    eq,
+    rq,
+    eh,
+    rh,
     itab,
     xst,
     gs,
@@ -83,8 +126,10 @@
     c_rcv,
     f_snd,
     f_rcv,
-    e_snd,
-    e_rcv,
+    q_snd,
+    q_rcv,
+    h_snd,
+    h_rcv,
     g_snd,
     g_rcv,
     o_sem,
@@ -158,7 +203,7 @@
     order = lax.broadcasted_iota(jnp.int32, (MODES, MODES), 0)
     place = lax.broadcasted_iota(jnp.int32, (MODES, MODES), 1)
     moved = jnp.where(order == ROWS * (place % NL) + place // NL, 1.0, 0.0).astype(BF)
-    hot = dot(jnp.where(morder[...] == order, 1.0, 0.0).astype(BF), moved)
+    hot = dot(jnp.where(morder[...].reshape(1, MODES) == order, 1.0, 0.0).astype(BF), moved)
     pick = hot.T.astype(BF)
 
     loads[0].wait()
@@ -208,7 +253,7 @@
         itab[:, reim * MODES : (reim + 1) * MODES] = dot(twt_v[reim], hot).astype(BF)
     loads[6].wait()
 
-    upper = lax.broadcasted_iota(jnp.int32, (NL, 8, CB), 1) < 4
+    sub = lax.broadcasted_iota(jnp.int32, (NL, 8, CB), 1)
 
     def analyse(k):
         got = rbuf[k].astype(F32)
@@ -234,69 +279,77 @@
     def synthesise(k):
         take(fr.at[k], f_rcv.at[k])
         back = dot(legt[k], fr[k].reshape(MODES, 2 * CB))
-        re = back[:, :CB].reshape(NL, 8, CB)
-        im = back[:, CB:].reshape(NL, 8, CB)
-        return (
-            jnp.where(upper, re, pltpu.roll(im, 4, 1)),
-            jnp.where(upper, pltpu.roll(re, 4, 1), im),
-        )
-
-    def pack(kp, first, second):
+        return back[:, :CB].reshape(NL, 8, CB), back[:, CB:].reshape(NL, 8, CB)
+
+    def gather(parts, first, n):
+        out = None
+        for i, part in enumerate(parts):
+            turned = pltpu.roll(part, (n * i - first) % 8, 1)
+            out = turned if out is None else jnp.where(sub < n * i, out, turned)
+        return out
+
+    def pack_quarters(backs):
+        for g in range(4):
+            tiles = [
+                gather([*backs[2 * i], *backs[2 * i + 1]], 2 * g, 2) for i in range(2)
+            ]
+            eq[g] = jnp.concatenate(tiles, axis=1).astype(BF)
+
+    def pack_halves(backs):
         for h in range(2):
-            es[h, kp] = jnp.concatenate([first[h], second[h]], axis=1).astype(BF)
-
-    def back_send(h, kp):
-        lat_send(es.at[h, kp], er.at[h, kp], e_snd.at[h, kp], e_rcv.at[h, kp])
-
-    def waves(h):
-        for kp in range(KP):
-            take(er.at[h, kp], e_rcv.at[h, kp])
-        xst[...] = er[h].astype(F32).reshape(KP * NL * 16, CB)
-        for q in range(2):
-            p = 2 * h + q
-            cols = []
-            for c in range(2):
-                cols.append(
-                    jnp.concatenate(
-                        [
-                            xst[
-                                pl.ds(kp * NL * 16 + k2 * 8 + reim * 4 + 2 * q + c, NL, stride=16),
-                                :,
-                            ]
-                            for reim in range(2)
-                            for kp in range(KP)
-                            for k2 in range(2)
-                        ],
-                        axis=0,
-                    ).astype(BF)
+            tiles = [gather(backs[i], 4 * h, 4) for i in range(2)]
+            eh[h] = jnp.concatenate(tiles, axis=1).astype(BF)
+
+    def send_quarter(g):
+        lat_send(eq.at[g], rq.at[g], q_snd.at[g], q_rcv.at[g])
+
+    def send_half(h):
+        lat_send(eh.at[h], rh.at[h], h_snd.at[h], h_rcv.at[h])
+
+    def waves(p):
+        take(rq.at[p], q_rcv.at[p])
+        if p % 2 == 0:
+            take(rh.at[p // 2], h_rcv.at[p // 2])
+        xst[: NL * 16] = rq[p].astype(F32).reshape(NL * 16, CB)
+        xst[NL * 16 :] = rh[p // 2].astype(F32).reshape(NL * 16, CB)
+        cols = []
+        for c in range(2):
+            part = []
+            for reim in range(2):
+                for k in range(4):
+                    part.append(xst[pl.ds(k * 4 + reim * 2 + c, NL, stride=16), :])
+                for k in range(2):
+                    at = NL * 16 + k * 8 + reim * 4 + 2 * (p % 2) + c
+                    part.append(xst[pl.ds(at, NL, stride=16), :])
+            cols.append(jnp.concatenate(part, axis=0).astype(BF))
+        wave = dot(itab[...], jnp.concatenate(cols, axis=1))
+        both = [grid_v[2 * p + c].astype(F32) + wave[:, c * CB : (c + 1) * CB] for c in range(2)]
+        for i in range(NX):
+            gs[p, i] = jnp.concatenate(
+                [b[i * LON : (i + 1) * LON] for b in both], axis=0
+            ).astype(BF)
+        for t, (pair, at, n) in enumerate(PIECES):
+            if pair == p:
+                part = pl.ds(at, n)
+                ch_send(
+                    gs.at[p, :, part], gr.at[p, :, part], g_snd.at[t], g_rcv.at[t]
                 )
-            wave = dot(itab[...], jnp.concatenate(cols, axis=1))
-            both = [grid_v[2 * p + c].astype(F32) + wave[:, c * CB : (c + 1) * CB] for c in range(2)]
-            for i in range(NX):
-                gs[p, i] = jnp.concatenate(
-                    [b[i * LON : (i + 1) * LON] for b in both], axis=0
-                ).astype(BF)
-            for t, (pair, at, n) in enumerate(PIECES):
-                if pair == p:
-                    part = pl.ds(at, n)
-                    ch_send(
-                        gs.at[p, :, part], gr.at[p, :, part], g_snd.at[t], g_rcv.at[t]
-                    )
+
 
     def points(t):
         p, at, n = PIECES[t]
         part = pl.ds(at, n)
         take(gr.at[p, :, part], g_rcv.at[t])
-        values = jnp.concatenate([gr[p, i, part, :] for i in range(NX)], axis=1).astype(F32)
-        center = jnp.mean(values, axis=-1, keepdims=True)
-        moved = values - center
-        spread = jnp.mean(moved * moved, axis=-1, keepdims=True)
-        normed = (moved * lax.rsqrt(spread + 1e-05) * lng[...]).astype(BF)
-        inner = dot(normed, win_v[...]) + bias[...]
-        hidden = jax.nn.gelu(inner, approximate=True).astype(BF)
-        ov[p, part, :] = (values + dot(hidden, wout_v[...])).astype(BF)
-        pltpu.make_async_copy(ov.at[p, part], out_h.at[p, part], o_sem.at[t]).start()
-
+        if t == len(PIECES) - 1:
+            copy = pltpu.make_async_copy(gr.at[p, :, part], last_h, o_sem.at[t])
+        else:
+            rows = jnp.concatenate([gr[p, i, part, :] for i in range(NX)], axis=1)
+            ov[p, part, :] = point_layer(rows, lng, win_v, bias, wout_v)
+            copy = pltpu.make_async_copy(ov.at[p, part], out_h.at[p, part], o_sem.at[t])
+        copy.start()
+        return copy
+
+    backs = []
     for kp in range(KP):
         a, b = 2 * kp, 2 * kp + 1
         take(rbuf.at[a], s_rcv.at[a])
@@ -305,33 +358,40 @@
         take(rbuf.at[b], s_rcv.at[b])
         analyse(b)
         if kp == KP - 1:
-            back_send(0, 0)
-            back_send(0, 1)
-        first = synthesise(a)
+            send_quarter(0)
+            send_quarter(1)
+        backs.append(synthesise(a))
         mix(b)
-        pack(kp, first, synthesise(b))
-    back_send(0, KP - 1)
-    for kp in range(KP):
-        back_send(1, kp)
+        backs.append(synthesise(b))
+        if kp == 1:
+            pack_quarters(backs)
+    pack_halves(backs[4:])
+    send_half(0)
+    send_half(1)
+    send_quarter(2)
+    send_quarter(3)
     loads[7].wait()
     loads[8].wait()
     waves(0)
-    points(0)
     waves(1)
-    for t in range(1, len(PIECES)):
-        points(t)
+    copies = [points(0)]
+    waves(2)
+    waves(3)
+    copies += [points(t) for t in range(1, len(PIECES))]
 
     for k in range(ROWS):
         take(sbuf.at[k, pl.ds(0, NL - 1)], s_snd.at[k])
         take(cs.at[k, pl.ds(0, NX - 1)], c_snd.at[k])
         take(fs.at[k, pl.ds(0, NX - 1)], f_snd.at[k])
-    for kp in range(KP):
-        for h in range(2):
-            take(es.at[h, kp, pl.ds(0, NL - 1)], e_snd.at[h, kp])
+    for g in range(4):
+        take(eq.at[g, pl.ds(0, NL - 1)], q_snd.at[g])
+    for h in range(2):
+        take(eh.at[h, pl.ds(0, NL - 1)], h_snd.at[h])
     for t, (p, at, n) in enumerate(PIECES):
         part = pl.ds(at, n)
         take(gs.at[p, pl.ds(0, NX - 1), part], g_snd.at[t])
-        pltpu.make_async_copy(ov.at[p, part], out_h.at[p, part], o_sem.at[t]).wait()
+    for copy in copies:
+        copy.wait()
 
 
 def body(
@@ -351,11 +411,14 @@
     vm = pl.BlockSpec(memory_space=pltpu.VMEM)
     hbm = pl.BlockSpec(memory_space=pl.ANY)
     dma = pltpu.SemaphoreType.DMA
-    out = pl.pallas_call(
+    part, last = pl.pallas_call(
         kernel,
-        out_shape=jax.ShapeDtypeStruct((CYC // 2, 2 * LON, NX * CB), BF),
+        out_shape=[
+            jax.ShapeDtypeStruct((CYC // 2, 2 * LON, NX * CB), BF),
+            jax.ShapeDtypeStruct((NX, PIECES[-1][2], CB), BF),
+        ],
         in_specs=[vm] * 4 + [hbm] * 9,
-        out_specs=hbm,
+        out_specs=[hbm] * 2,
         scratch_shapes=[
             pltpu.VMEM((CYC, NLON, CB), BF),
             pltpu.VMEM((2, MODES, NLON), BF),
@@ -375,10 +438,12 @@
             pltpu.VMEM((2 * NX * CB, 2 * NX * CB), BF),
             pltpu.VMEM((ROWS, NX, LB, 2 * CB), BF),
             pltpu.VMEM((ROWS, NX, LB, 2 * CB), BF),
-            pltpu.VMEM((2, KP, NL, 16, CB), BF),
-            pltpu.VMEM((2, KP, NL, 16, CB), BF),
+            pltpu.VMEM((4, NL, 16, CB), BF),
+            pltpu.VMEM((4, NL, 16, CB), BF),
+            pltpu.VMEM((2, NL, 16, CB), BF),
+            pltpu.VMEM((2, NL, 16, CB), BF),
             pltpu.VMEM((NLON, 2 * MODES), BF),
-            pltpu.VMEM((KP * NL * 16, CB), F32),
+            pltpu.VMEM((2 * NL * 16, CB), F32),
             pltpu.VMEM((CYC // 2, NX, 2 * LON, CB), BF),
             pltpu.VMEM((CYC // 2, NX, 2 * LON, CB), BF),
             pltpu.VMEM((CYC // 2, 2 * LON, NX * CB), BF),
@@ -389,8 +454,10 @@
             dma((ROWS,)),
             dma((ROWS,)),
             dma((ROWS,)),
-            dma((2, KP)),
-            dma((2, KP)),
+            dma((4,)),
+            dma((4,)),
+            dma((2,)),
+            dma((2,)),
             dma((len(PIECES),)),
             dma((len(PIECES),)),
             dma((len(PIECES),)),
@@ -400,7 +467,7 @@
         ),
         name="sfno_block",
     )(
-        m_order[None, :],
+        m_order,
         quad_weights[None, :],
         ln_gain[None, :],
         mlp_bias[None, :],
@@ -414,6 +481,23 @@
         mlp_in,
         mlp_out,
     )
+    out = pl.pallas_call(
+        finish,
+        out_shape=jax.ShapeDtypeStruct(part.shape, BF),
+        in_specs=[vm] * 2 + [hbm] * 4,
+        out_specs=hbm,
+        scratch_shapes=[
+            pltpu.VMEM(mlp_in.shape, BF),
+            pltpu.VMEM(mlp_out.shape, BF),
+            pltpu.VMEM(last.shape, BF),
+            pltpu.VMEM(part.shape, BF),
+            dma((3,)),
+            dma((len(PIECES),)),
+            dma((len(PIECES),)),
+        ],
+        compiler_params=pltpu.CompilerParams(vmem_limit_bytes=60 << 20),
+        name="last_points",
+    )(ln_gain[None, :], mlp_bias[None, :], mlp_in, mlp_out, last, part)
     return out.reshape(CYC, LON, NX * CB)
 
 

time: 127 us -> 127 us (level)
  Pallas kernels: 122 us -> 127 us
  local copies, waits for them, and re-layouts: 4.87 us -> 0 us
    pallas_call x1 -> x2, Pallas kernels: 122 us -> 127 us  [the longest x1 121 us: body(): pl.pallas_call(kernel, out_shape=[jax.ShapeDtypeStruct((CYC // 2, 2 * LON...]
    unnamed x1 -> x0, local copies, waits for them, and re-layouts: 3.62 us -> none
where the time goes in v3:
time: 127 us
  Pallas kernels  127 us (100%)
    pallas_call x1, Pallas kernels, body(): pl.pallas_call(kernel, out_shape=[jax.ShapeDtypeStruct((CYC // 2, 2 * LON...  121 us
    pallas_call x1, Pallas kernels, body(): pl.pallas_call(finish, out_shape=jax.ShapeDtypeStruct(part.shape, BF), in...  5.94 us

profile of v3, /device:TPU:1, one launch (start us, length us, event | category | flops | bytes accessed | tf_op | source)
XLA Modules:
  0.0 126.8 jit_solution(6653666292631530685)
XLA Ops:
  0.0 120.7 %sfno_block.1 = (bf16[4,720,512]{2,1,0:T(8,128)(2,1)}, bf16[4,352,128]{2,1,0:T(8,128)(2,1)}) custom-call(s32[384]{0:T(512)} %morder.1, f32[1,512]{1,0:T(1,128)} %bitcast.8, f32[1,512]{1,0:T(1,128)} %bitcast.6, f32[1,1024]{1,0:T(1,128)} %bitcast.4, bf16[8,1440,128]{2,1,0:T(8,128)(2,1)} %grid_h.1, bf16[2,384,1440]{2,1,0:T(8,128)(2,1)} %constant.4.clone.tw_h, ...), custom_call_target="tpu_custom_call" | custom-call | tf_op jit(solution)/shard_map/sfno_block/pallas_call | solution.py:414
  120.7 5.9 %last_points.1 = bf16[4,720,512]{2,1,0:T(8,128)(2,1)} custom-call(f32[1,512]{1,0:T(1,128)} %bitcast.7, f32[1,1024]{1,0:T(1,128)} %bitcast.5, bf16[512,1024]{1,0:T(8,128)(2,1)} %win_h.3, bf16[1024,512]{1,0:T(8,128)(2,1)} %wout_h.3, bf16[4,352,128]{2,1,0:T(8,128)(2,1)} %get-tuple-element.7.last_h, bf16[4,720,512]{2,1,0:T(8,128)(2,1)} %get-tuple-element.8.part_h), custom_call_target="tpu_custom_call" | custom-call | tf_op jit(solution)/shard_map/last_points/pallas_call | solution.py:484

commit v4 on v3

--- a/solution.py
+++ b/solution.py
@@ -19,7 +19,7 @@
 LB = MODES // NX
 LON = NLON // NX
 KP = ROWS // 2
-PIECES = [(0, 0, 720), (1, 0, 720), (2, 0, 720), (3, 0, 368), (3, 368, 352)]
+PIECES = [(0, 0, 720), (1, 0, 720), (2, 0, 720), (3, 0, 256), (3, 256, 256), (3, 512, 208)]
 MESH = pl.DeviceIdType.MESH
 BF = jnp.bfloat16
 F32 = jnp.float32
@@ -43,37 +43,24 @@
     spread = jnp.mean(moved * moved, axis=-1, keepdims=True)
     normed = (moved * lax.rsqrt(spread + 1e-05) * lng[...]).astype(BF)
     inner = dot(normed, win[...]) + bias[...]
-    hidden = jax.nn.gelu(inner, approximate=True).astype(BF)
+    half = 0.5 * inner
+    root = math.sqrt(2.0 / math.pi)
+    bent = jnp.tanh(inner * (root + (root * 0.044715) * (inner * inner)))
+    hidden = (half + half * bent).astype(BF)
     return (values + dot(hidden, wout[...])).astype(BF)
 
 
-def finish(lng, bias, win_h, wout_h, last_h, part_h, out_h, win, wout, last, hold, l_sem, i_sem, o_sem):
-    p, at, n = PIECES[-1]
-    loads = [
-        pltpu.make_async_copy(src, dst, l_sem.at[i])
-        for i, (src, dst) in enumerate([(last_h, last), (win_h, win), (wout_h, wout)])
-    ]
-    for load in loads:
-        load.start()
-
-    def move(t, src, dst, sem):
-        pair, first, rows = PIECES[t]
-        part = pl.ds(first, rows)
-        return pltpu.make_async_copy(src.at[pair, part], dst.at[pair, part], sem.at[t])
-
-    others = range(len(PIECES) - 1)
-    for t in others:
-        move(t, part_h, hold, i_sem).start()
-    for t in others:
-        move(t, part_h, hold, i_sem).wait()
-        move(t, hold, out_h, o_sem).start()
-    for load in loads:
-        load.wait()
-    rows = jnp.concatenate([last[i] for i in range(NX)], axis=1)
-    hold[p, at : at + n, :] = point_layer(rows, lng, win, bias, wout)
-    move(len(PIECES) - 1, hold, out_h, o_sem).start()
-    for t in range(len(PIECES)):
-        move(t, hold, out_h, o_sem).wait()
+def finish(part_h, out_h, hold, i_sem, o_sem):
+    pairs = range(CYC // 2)
+    into = [pltpu.make_async_copy(part_h.at[p], hold.at[p], i_sem.at[p]) for p in pairs]
+    out = [pltpu.make_async_copy(hold.at[p], out_h.at[p], o_sem.at[p]) for p in pairs]
+    for copy in into:
+        copy.start()
+    for p in pairs:
+        into[p].wait()
+        out[p].start()
+    for copy in out:
+        copy.wait()
 
 
 def kernel(
@@ -91,7 +78,6 @@
     win_h,
     wout_h,
     out_h,
-    last_h,
     grid_v,
     tw_v,
     twt_v,
@@ -340,31 +326,26 @@
         p, at, n = PIECES[t]
         part = pl.ds(at, n)
         take(gr.at[p, :, part], g_rcv.at[t])
-        if t == len(PIECES) - 1:
-            copy = pltpu.make_async_copy(gr.at[p, :, part], last_h, o_sem.at[t])
-        else:
-            rows = jnp.concatenate([gr[p, i, part, :] for i in range(NX)], axis=1)
-            ov[p, part, :] = point_layer(rows, lng, win_v, bias, wout_v)
-            copy = pltpu.make_async_copy(ov.at[p, part], out_h.at[p, part], o_sem.at[t])
+        rows = jnp.concatenate([gr[p, i, part, :] for i in range(NX)], axis=1)
+        ov[p, part, :] = point_layer(rows, lng, win_v, bias, wout_v)
+        copy = pltpu.make_async_copy(ov.at[p, part], out_h.at[p, part], o_sem.at[t])
         copy.start()
         return copy
 
     backs = []
-    for kp in range(KP):
-        a, b = 2 * kp, 2 * kp + 1
-        take(rbuf.at[a], s_rcv.at[a])
-        analyse(a)
-        mix(a)
-        take(rbuf.at[b], s_rcv.at[b])
-        analyse(b)
-        if kp == KP - 1:
-            send_quarter(0)
-            send_quarter(1)
-        backs.append(synthesise(a))
-        mix(b)
-        backs.append(synthesise(b))
-        if kp == 1:
-            pack_quarters(backs)
+    for k in range(ROWS):
+        take(rbuf.at[k], s_rcv.at[k])
+        analyse(k)
+        if k >= 1:
+            mix(k - 1)
+        if k >= 2:
+            backs.append(synthesise(k - 2))
+    pack_quarters(backs)
+    send_quarter(0)
+    send_quarter(1)
+    mix(ROWS - 1)
+    backs.append(synthesise(ROWS - 2))
+    backs.append(synthesise(ROWS - 1))
     pack_halves(backs[4:])
     send_half(0)
     send_half(1)
@@ -411,14 +392,11 @@
     vm = pl.BlockSpec(memory_space=pltpu.VMEM)
     hbm = pl.BlockSpec(memory_space=pl.ANY)
     dma = pltpu.SemaphoreType.DMA
-    part, last = pl.pallas_call(
+    part = pl.pallas_call(
         kernel,
-        out_shape=[
-            jax.ShapeDtypeStruct((CYC // 2, 2 * LON, NX * CB), BF),
-            jax.ShapeDtypeStruct((NX, PIECES[-1][2], CB), BF),
-        ],
+        out_shape=jax.ShapeDtypeStruct((CYC // 2, 2 * LON, NX * CB), BF),
         in_specs=[vm] * 4 + [hbm] * 9,
-        out_specs=[hbm] * 2,
+        out_specs=hbm,
         scratch_shapes=[
             pltpu.VMEM((CYC, NLON, CB), BF),
             pltpu.VMEM((2, MODES, NLON), BF),
@@ -484,20 +462,16 @@
     out = pl.pallas_call(
         finish,
         out_shape=jax.ShapeDtypeStruct(part.shape, BF),
-        in_specs=[vm] * 2 + [hbm] * 4,
+        in_specs=[hbm],
         out_specs=hbm,
         scratch_shapes=[
-            pltpu.VMEM(mlp_in.shape, BF),
-            pltpu.VMEM(mlp_out.shape, BF),
-            pltpu.VMEM(last.shape, BF),
             pltpu.VMEM(part.shape, BF),
-            dma((3,)),
-            dma((len(PIECES),)),
-            dma((len(PIECES),)),
+            dma((CYC // 2,)),
+            dma((CYC // 2,)),
         ],
         compiler_params=pltpu.CompilerParams(vmem_limit_bytes=60 << 20),
-        name="last_points",
-    )(ln_gain[None, :], mlp_bias[None, :], mlp_in, mlp_out, last, part)
+        name="move_result",
+    )(part)
     return out.reshape(CYC, LON, NX * CB)
 
 

time: 127 us -> 115 us (0.906)
  Pallas kernels: 127 us -> 115 us
    pallas_call x1, Pallas kernels: 121 us -> 112 us  [body(): pl.pallas_call(kernel, out_shape=jax.ShapeDtypeStruct((CYC // 2, 2 * LON,...]
    pallas_call x1, Pallas kernels: 5.94 us -> 2.78 us  [body(): pl.pallas_call(finish, out_shape=jax.ShapeDtypeStruct(part.shape, BF), in...]
where the time goes in v4:
time: 115 us
  Pallas kernels  115 us (100%)
    pallas_call x1, Pallas kernels, body(): pl.pallas_call(kernel, out_shape=jax.ShapeDtypeStruct((CYC // 2, 2 * LON,...  112 us
    pallas_call x1, Pallas kernels, body(): pl.pallas_call(finish, out_shape=jax.ShapeDtypeStruct(part.shape, BF), in...  2.78 us

profile of v4, /device:TPU:1, one launch (start us, length us, event | category | flops | bytes accessed | tf_op | source)
XLA Modules:
  0.0 115.0 jit_solution(8167792286227560866)
XLA Ops:
  0.0 112.0 %sfno_block.1.part_h = bf16[4,720,512]{2,1,0:T(8,128)(2,1)} custom-call(s32[384]{0:T(512)} %morder.1, f32[1,512]{1,0:T(1,128)} %bitcast.5, f32[1,512]{1,0:T(1,128)} %bitcast.6, f32[1,1024]{1,0:T(1,128)} %bitcast.4, bf16[8,1440,128]{2,1,0:T(8,128)(2,1)} %grid_h.1, bf16[2,384,1440]{2,1,0:T(8,128)(2,1)} %constant.4.clone.tw_h, ...), custom_call_target="tpu_custom_call" | custom-call | tf_op jit(solution)/shard_map/sfno_block/pallas_call | solution.py:395
  112.0 2.8 %move_result.1 = bf16[4,720,512]{2,1,0:T(8,128)(2,1)} custom-call(bf16[4,720,512]{2,1,0:T(8,128)(2,1)} %sfno_block.1.part_h), custom_call_target="tpu_custom_call" | custom-call | tf_op jit(solution)/shard_map/move_result/pallas_call | solution.py:462

commit v5 on v4

--- a/solution.py
+++ b/solution.py
@@ -17,6 +17,7 @@
 ROWS = 6
 CB = 128
 LB = MODES // NX
+LQ = NL // NX
 LON = NLON // NX
 KP = ROWS // 2
 PIECES = [(0, 0, 720), (1, 0, 720), (2, 0, 720), (3, 0, 256), (3, 256, 256), (3, 512, 208)]
@@ -86,11 +87,15 @@
     mr_v,
     mi_v,
     gain_v,
+    gaind_v,
     win_v,
     wout_v,
     stage,
     sbuf,
     rbuf,
+    mr_in,
+    mr_out,
+    sb2,
     cs,
     cr,
     wm,
@@ -108,6 +113,8 @@
     load_sem,
     s_snd,
     s_rcv,
+    m_snd,
+    m_rcv,
     c_snd,
     c_rcv,
     f_snd,
@@ -129,11 +136,12 @@
             [
                 (tw_h, tw_v),
                 (grid_h, grid_v),
-                (leg_h, leg_v),
                 (mr_h, mr_v),
                 (mi_h, mi_v),
+                (leg_h, leg_v),
                 (twt_h, twt_v),
                 (gain_h.at[pl.ds(pl.multiple_of(x * LB, LB), LB)], gain_v),
+                (gain_h.at[:, pl.ds(pl.multiple_of(x * CB, CB), CB)], gaind_v),
                 (win_h, win_v),
                 (wout_h, wout_v),
             ]
@@ -174,14 +182,14 @@
         for s in (2, 1, 3):
             i = lax.rem(x + s, NX)
             pltpu.make_async_remote_copy(
-                src_ref=src.at[i],
-                dst_ref=dst.at[x],
+                src_ref=src(i),
+                dst_ref=dst,
                 send_sem=snd,
                 recv_sem=rcv,
                 device_id=(me, i),
                 device_id_type=MESH,
             ).start()
-        pltpu.make_async_copy(src.at[x], dst.at[x], rcv).start()
+        pltpu.make_async_copy(src(x), dst, rcv).start()
 
     def take(ref, sem):
         pltpu.make_async_copy(ref, ref, sem).wait()
@@ -194,7 +202,8 @@
 
     loads[0].wait()
     loads[1].wait()
-    for kp in range(KP):
+
+    def fourier(kp):
         rows = pick[kp * 2 * NL : (kp + 1) * 2 * NL]
         table = jnp.concatenate(
             [dot(rows, tw_v[0]).astype(BF), dot(rows, tw_v[1]).astype(BF)], axis=0
@@ -212,18 +221,26 @@
         for k2 in range(2):
             part = stage[k2 * NL * 16 : (k2 + 1) * NL * 16]
             sbuf[2 * kp + k2] = part.astype(BF).reshape(NL, 16, CB)
-        if kp == 0:
-            pl.semaphore_wait(barrier, NL - 1 + NX - 1)
-        for k in (2 * kp, 2 * kp + 1):
-            lat_send(sbuf.at[k], rbuf.at[k], s_snd.at[k], s_rcv.at[k])
-
+
+    def spectra_send(src, k):
+        lat_send(src, rbuf.at[k], s_snd.at[k], s_rcv.at[k])
+
+    def split(tiles):
+        tiles = tiles.astype(F32)
+        n = tiles.shape[0] * 8
+        return [tiles[:, i * 8 : (i + 1) * 8, :].reshape(n, CB).astype(BF) for i in range(2)]
+
+    fourier(0)
+    pl.semaphore_wait(barrier, NL - 1 + NX - 1)
+    spectra_send(sbuf.at[0], 0)
+    spectra_send(sbuf.at[1], 1)
+
+    fourier(2)
+    ch_send(
+        lambda i: sbuf.at[pl.ds(4, 2), pl.ds(i * LQ, LQ)], mr_in.at[x], m_snd.at[0], m_rcv.at[0]
+    )
     loads[2].wait()
-    for k in range(ROWS):
-        values = leg_v[k]
-        legt[k] = values.T
-        leg_v[k] = (values.astype(F32) * quad[...]).astype(BF)
     loads[3].wait()
-    loads[4].wait()
     for xs in range(NX):
         for xd in range(NX):
             re = mr_v[xs * CB : (xs + 1) * CB, xd * CB : (xd + 1) * CB]
@@ -233,25 +250,44 @@
             wm[r0 : r0 + CB, c0 + CB : c0 + 2 * CB] = im
             wm[r0 + CB : r0 + 2 * CB, c0 : c0 + CB] = -im
             wm[r0 + CB : r0 + 2 * CB, c0 + CB : c0 + 2 * CB] = re
+    fourier(1)
+    spectra_send(sbuf.at[2], 2)
+    spectra_send(sbuf.at[3], 3)
+
+    take(mr_in, m_rcv.at[0])
+    lhs = []
+    for i in range(NX):
+        lhs += split(mr_in[i].reshape(2 * LQ, 16, CB))
+    res = dot(jnp.concatenate(lhs, axis=1), wm[...])
+    for i in range(NX):
+        part = [
+            res[:, (2 * i + reim) * CB : (2 * i + reim + 1) * CB].reshape(2 * LQ, 8, CB)
+            for reim in range(2)
+        ]
+        mr_out[i] = jnp.concatenate(part, axis=1).astype(BF).reshape(2, LQ, 16, CB)
+    ch_send(lambda i: mr_out.at[i], sb2.at[:, pl.ds(x * LQ, LQ)], m_snd.at[1], m_rcv.at[1])
+
+    loads[4].wait()
+    for k in range(ROWS):
+        values = leg_v[k]
+        legt[k] = values.T
+        leg_v[k] = (values.astype(F32) * quad[...]).astype(BF)
     loads[5].wait()
     hot = (hot * jnp.where(order == 0, 1.0, 2.0)).astype(BF)
     for reim in range(2):
         itab[:, reim * MODES : (reim + 1) * MODES] = dot(twt_v[reim], hot).astype(BF)
     loads[6].wait()
+    loads[7].wait()
 
     sub = lax.broadcasted_iota(jnp.int32, (NL, 8, CB), 1)
 
     def analyse(k):
-        got = rbuf[k].astype(F32)
-        spec = jnp.concatenate(
-            [
-                got[:, :8, :].reshape(NL * 8, CB).astype(BF),
-                got[:, 8:, :].reshape(NL * 8, CB).astype(BF),
-            ],
-            axis=1,
-        )
-        cs[k] = dot(leg_v[k], spec).astype(BF).reshape(NX, LB, 2 * CB)
-        ch_send(cs.at[k], cr.at[k], c_snd.at[k], c_rcv.at[k])
+        take(rbuf.at[k], s_rcv.at[k])
+        return dot(leg_v[k], jnp.concatenate(split(rbuf[k]), axis=1))
+
+    def offer(k):
+        cs[k] = analyse(k).astype(BF).reshape(NX, LB, 2 * CB)
+        ch_send(lambda i: cs.at[k, i], cr.at[k, x], c_snd.at[k], c_rcv.at[k])
 
     def mix(k):
         take(cr.at[k], c_rcv.at[k])
@@ -260,12 +296,19 @@
             part = gain_v[:, i * CB : (i + 1) * CB]
             part = jnp.concatenate([part, part], axis=1)
             fs[k, i] = (res[:, i * 2 * CB : (i + 1) * 2 * CB] * part).astype(BF)
-        ch_send(fs.at[k], fr.at[k], f_snd.at[k], f_rcv.at[k])
-
-    def synthesise(k):
+        ch_send(lambda i: fs.at[k, i], fr.at[k, x], f_snd.at[k], f_rcv.at[k])
+
+    def synthesise(k, filt):
+        back = dot(legt[k], filt)
+        return back[:, :CB].reshape(NL, 8, CB), back[:, CB:].reshape(NL, 8, CB)
+
+    def received(k):
         take(fr.at[k], f_rcv.at[k])
-        back = dot(legt[k], fr[k].reshape(MODES, 2 * CB))
-        return back[:, :CB].reshape(NL, 8, CB), back[:, CB:].reshape(NL, 8, CB)
+        return fr[k].reshape(MODES, 2 * CB)
+
+    def filtered(k):
+        gain = gaind_v[...]
+        return (analyse(k) * jnp.concatenate([gain, gain], axis=1)).astype(BF)
 
     def gather(parts, first, n):
         out = None
@@ -318,7 +361,7 @@
             if pair == p:
                 part = pl.ds(at, n)
                 ch_send(
-                    gs.at[p, :, part], gr.at[p, :, part], g_snd.at[t], g_rcv.at[t]
+                    lambda i: gs.at[p, i, part], gr.at[p, x, part], g_snd.at[t], g_rcv.at[t]
                 )
 
 
@@ -332,27 +375,31 @@
         copy.start()
         return copy
 
-    backs = []
-    for k in range(ROWS):
-        take(rbuf.at[k], s_rcv.at[k])
-        analyse(k)
-        if k >= 1:
-            mix(k - 1)
-        if k >= 2:
-            backs.append(synthesise(k - 2))
+    offer(0)
+    offer(1)
+    mix(0)
+    take(sb2, m_rcv.at[1])
+    spectra_send(sb2.at[0], 4)
+    spectra_send(sb2.at[1], 5)
+    offer(2)
+    mix(1)
+    backs = [synthesise(0, received(0))]
+    offer(3)
+    mix(2)
+    backs.append(synthesise(1, received(1)))
+    backs.append(synthesise(2, received(2)))
+    mix(3)
+    backs.append(synthesise(3, received(3)))
     pack_quarters(backs)
     send_quarter(0)
+    pack_halves([synthesise(k, filtered(k)) for k in (4, 5)])
+    send_half(0)
     send_quarter(1)
-    mix(ROWS - 1)
-    backs.append(synthesise(ROWS - 2))
-    backs.append(synthesise(ROWS - 1))
-    pack_halves(backs[4:])
-    send_half(0)
     send_half(1)
     send_quarter(2)
     send_quarter(3)
-    loads[7].wait()
     loads[8].wait()
+    loads[9].wait()
     waves(0)
     waves(1)
     copies = [points(0)]
@@ -362,8 +409,11 @@
 
     for k in range(ROWS):
         take(sbuf.at[k, pl.ds(0, NL - 1)], s_snd.at[k])
+    for k in range(4):
         take(cs.at[k, pl.ds(0, NX - 1)], c_snd.at[k])
         take(fs.at[k, pl.ds(0, NX - 1)], f_snd.at[k])
+    for i in range(2):
+        take(mr_out.at[pl.ds(0, NX - 1)], m_snd.at[i])
     for g in range(4):
         take(eq.at[g, pl.ds(0, NL - 1)], q_snd.at[g])
     for h in range(2):
@@ -406,16 +456,20 @@
             pltpu.VMEM(mix_real.shape, BF),
             pltpu.VMEM(mix_imag.shape, BF),
             pltpu.VMEM((LB, NX * CB), F32),
+            pltpu.VMEM((MODES, CB), F32),
             pltpu.VMEM(mlp_in.shape, BF),
             pltpu.VMEM(mlp_out.shape, BF),
             pltpu.VMEM((NL * 32, CB), F32),
             pltpu.VMEM((ROWS, NL, 16, CB), BF),
             pltpu.VMEM((ROWS, NL, 16, CB), BF),
-            pltpu.VMEM((ROWS, NX, LB, 2 * CB), BF),
-            pltpu.VMEM((ROWS, NX, LB, 2 * CB), BF),
+            pltpu.VMEM((NX, 2, LQ, 16, CB), BF),
+            pltpu.VMEM((NX, 2, LQ, 16, CB), BF),
+            pltpu.VMEM((2, NL, 16, CB), BF),
+            pltpu.VMEM((4, NX, LB, 2 * CB), BF),
+            pltpu.VMEM((4, NX, LB, 2 * CB), BF),
             pltpu.VMEM((2 * NX * CB, 2 * NX * CB), BF),
-            pltpu.VMEM((ROWS, NX, LB, 2 * CB), BF),
-            pltpu.VMEM((ROWS, NX, LB, 2 * CB), BF),
+            pltpu.VMEM((4, NX, LB, 2 * CB), BF),
+            pltpu.VMEM((4, NX, LB, 2 * CB), BF),
             pltpu.VMEM((4, NL, 16, CB), BF),
             pltpu.VMEM((4, NL, 16, CB), BF),
             pltpu.VMEM((2, NL, 16, CB), BF),
@@ -425,13 +479,15 @@
             pltpu.VMEM((CYC // 2, NX, 2 * LON, CB), BF),
             pltpu.VMEM((CYC // 2, NX, 2 * LON, CB), BF),
             pltpu.VMEM((CYC // 2, 2 * LON, NX * CB), BF),
-            dma((9,)),
+            dma((10,)),
             dma((ROWS,)),
             dma((ROWS,)),
-            dma((ROWS,)),
-            dma((ROWS,)),
-            dma((ROWS,)),
-            dma((ROWS,)),
+            dma((2,)),
+            dma((2,)),
+            dma((4,)),
+            dma((4,)),
+            dma((4,)),
+            dma((4,)),
             dma((4,)),
             dma((4,)),
             dma((2,)),

time: 115 us -> 110 us (0.957)
  Pallas kernels: 115 us -> 110 us
    pallas_call x1, Pallas kernels: 112 us -> 107 us  [body(): pl.pallas_call(kernel, out_shape=jax.ShapeDtypeStruct((CYC // 2, 2 * LON,...]
where the time goes in v5:
time: 110 us
  Pallas kernels  110 us (100%)
    pallas_call x1, Pallas kernels, body(): pl.pallas_call(kernel, out_shape=jax.ShapeDtypeStruct((CYC // 2, 2 * LON,...  107 us
    pallas_call x1, Pallas kernels, body(): pl.pallas_call(finish, out_shape=jax.ShapeDtypeStruct(part.shape, BF), in...  2.78 us

profile of v5, /device:TPU:1, one launch (start us, length us, event | category | flops | bytes accessed | tf_op | source)
XLA Modules:
  0.0 110.3 jit_solution(14138833418653720677)
XLA Ops:
  0.0 107.4 %sfno_block.1.part_h = bf16[4,720,512]{2,1,0:T(8,128)(2,1)} custom-call(s32[384]{0:T(512)} %morder.1, f32[1,512]{1,0:T(1,128)} %bitcast.5, f32[1,512]{1,0:T(1,128)} %bitcast.6, f32[1,1024]{1,0:T(1,128)} %bitcast.4, bf16[8,1440,128]{2,1,0:T(8,128)(2,1)} %grid_h.1, bf16[2,384,1440]{2,1,0:T(8,128)(2,1)} %constant.4.clone.tw_h, ...), custom_call_target="tpu_custom_call" | custom-call | tf_op jit(solution)/shard_map/sfno_block/pallas_call | solution.py:445
  107.4 2.8 %move_result.1 = bf16[4,720,512]{2,1,0:T(8,128)(2,1)} custom-call(bf16[4,720,512]{2,1,0:T(8,128)(2,1)} %sfno_block.1.part_h), custom_call_target="tpu_custom_call" | custom-call | tf_op jit(solution)/shard_map/move_result/pallas_call | solution.py:518

commit v6 on v5

--- a/solution.py
+++ b/solution.py
@@ -233,12 +233,12 @@
     fourier(0)
     pl.semaphore_wait(barrier, NL - 1 + NX - 1)
     spectra_send(sbuf.at[0], 0)
-    spectra_send(sbuf.at[1], 1)
 
     fourier(2)
     ch_send(
         lambda i: sbuf.at[pl.ds(4, 2), pl.ds(i * LQ, LQ)], mr_in.at[x], m_snd.at[0], m_rcv.at[0]
     )
+    spectra_send(sbuf.at[1], 1)
     loads[2].wait()
     loads[3].wait()
     for xs in range(NX):
@@ -376,11 +376,11 @@
         return copy
 
     offer(0)
-    offer(1)
-    mix(0)
     take(sb2, m_rcv.at[1])
     spectra_send(sb2.at[0], 4)
     spectra_send(sb2.at[1], 5)
+    offer(1)
+    mix(0)
     offer(2)
     mix(1)
     backs = [synthesise(0, received(0))]

time: 110 us -> 111 us (level)
  no operation moved by 1% of the time
where the time goes in v6:
time: 111 us; the launch traced here: 110 us
  Pallas kernels  110 us (99%)
    pallas_call x1, Pallas kernels, body(): pl.pallas_call(kernel, out_shape=jax.ShapeDtypeStruct((CYC // 2, 2 * LON,...  107 us
    pallas_call x1, Pallas kernels, body(): pl.pallas_call(finish, out_shape=jax.ShapeDtypeStruct(part.shape, BF), in...  2.78 us

profile of v6, /device:TPU:1, one launch (start us, length us, event | category | flops | bytes accessed | tf_op | source)
XLA Modules:
  0.0 110.4 jit_solution(15250623482137815379)
XLA Ops:
  0.0 107.5 %sfno_block.1.part_h = bf16[4,720,512]{2,1,0:T(8,128)(2,1)} custom-call(s32[384]{0:T(512)} %morder.1, f32[1,512]{1,0:T(1,128)} %bitcast.5, f32[1,512]{1,0:T(1,128)} %bitcast.6, f32[1,1024]{1,0:T(1,128)} %bitcast.4, bf16[8,1440,128]{2,1,0:T(8,128)(2,1)} %grid_h.1, bf16[2,384,1440]{2,1,0:T(8,128)(2,1)} %constant.4.clone.tw_h, ...), custom_call_target="tpu_custom_call" | custom-call | tf_op jit(solution)/shard_map/sfno_block/pallas_call | solution.py:445
  107.5 2.8 %move_result.1 = bf16[4,720,512]{2,1,0:T(8,128)(2,1)} custom-call(bf16[4,720,512]{2,1,0:T(8,128)(2,1)} %sfno_block.1.part_h), custom_call_target="tpu_custom_call" | custom-call | tf_op jit(solution)/shard_map/move_result/pallas_call | solution.py:518

commit v7 on v6

--- a/solution.py
+++ b/solution.py
@@ -194,33 +194,35 @@
     def take(ref, sem):
         pltpu.make_async_copy(ref, ref, sem).wait()
 
-    order = lax.broadcasted_iota(jnp.int32, (MODES, MODES), 0)
-    place = lax.broadcasted_iota(jnp.int32, (MODES, MODES), 1)
-    moved = jnp.where(order == ROWS * (place % NL) + place // NL, 1.0, 0.0).astype(BF)
-    hot = dot(jnp.where(morder[...].reshape(1, MODES) == order, 1.0, 0.0).astype(BF), moved)
-    pick = hot.T.astype(BF)
+    column = jnp.broadcast_to(morder[...].reshape(1, MODES).astype(F32), (8, MODES)).T[:, :1]
+    lane = lax.broadcasted_iota(jnp.int32, (MODES, MODES), 1)
+    hot = jnp.where(column.astype(jnp.int32) == lane, 1.0, 0.0).astype(BF)
 
     loads[0].wait()
     loads[1].wait()
 
-    def fourier(kp):
-        rows = pick[kp * 2 * NL : (kp + 1) * 2 * NL]
+    def fourier(ks):
+        n = len(ks)
+        at = lax.broadcasted_iota(jnp.int32, (n * NL, MODES), 0)
+        at = ROWS * (at & (NL - 1)) + ks[0] + (at >> 6)
+        wanted = jnp.where(at == lane[: n * NL], 1.0, 0.0).astype(BF)
+        pick = dot(wanted, hot).astype(BF)
         table = jnp.concatenate(
-            [dot(rows, tw_v[0]).astype(BF), dot(rows, tw_v[1]).astype(BF)], axis=0
+            [dot(pick, tw_v[0]).astype(BF), dot(pick, tw_v[1]).astype(BF)], axis=0
         )
         for p in range(CYC // 2):
             res = dot(table, jnp.concatenate([grid_v[2 * p], grid_v[2 * p + 1]], axis=1))
             for reim in range(2):
-                for k2 in range(2):
-                    at = (reim * 2 + k2) * NL
+                for k2 in range(n):
+                    first = (reim * n + k2) * NL
                     for c in range(2):
                         row = k2 * NL * 16 + reim * 8 + 2 * p + c
                         stage[pl.ds(row, NL, stride=16), :] = res[
-                            at : at + NL, c * CB : (c + 1) * CB
+                            first : first + NL, c * CB : (c + 1) * CB
                         ]
-        for k2 in range(2):
+        for k2 in range(n):
             part = stage[k2 * NL * 16 : (k2 + 1) * NL * 16]
-            sbuf[2 * kp + k2] = part.astype(BF).reshape(NL, 16, CB)
+            sbuf[ks[k2]] = part.astype(BF).reshape(NL, 16, CB)
 
     def spectra_send(src, k):
         lat_send(src, rbuf.at[k], s_snd.at[k], s_rcv.at[k])
@@ -230,14 +232,15 @@
         n = tiles.shape[0] * 8
         return [tiles[:, i * 8 : (i + 1) * 8, :].reshape(n, CB).astype(BF) for i in range(2)]
 
-    fourier(0)
+    fourier((0,))
     pl.semaphore_wait(barrier, NL - 1 + NX - 1)
     spectra_send(sbuf.at[0], 0)
 
-    fourier(2)
+    fourier((4, 5))
     ch_send(
         lambda i: sbuf.at[pl.ds(4, 2), pl.ds(i * LQ, LQ)], mr_in.at[x], m_snd.at[0], m_rcv.at[0]
     )
+    fourier((1,))
     spectra_send(sbuf.at[1], 1)
     loads[2].wait()
     loads[3].wait()
@@ -250,7 +253,7 @@
             wm[r0 : r0 + CB, c0 + CB : c0 + 2 * CB] = im
             wm[r0 + CB : r0 + 2 * CB, c0 : c0 + CB] = -im
             wm[r0 + CB : r0 + 2 * CB, c0 + CB : c0 + 2 * CB] = re
-    fourier(1)
+    fourier((2, 3))
     spectra_send(sbuf.at[2], 2)
     spectra_send(sbuf.at[3], 3)
 
@@ -273,9 +276,13 @@
         legt[k] = values.T
         leg_v[k] = (values.astype(F32) * quad[...]).astype(BF)
     loads[5].wait()
-    hot = (hot * jnp.where(order == 0, 1.0, 2.0)).astype(BF)
+    order = lax.broadcasted_iota(jnp.int32, (MODES, MODES), 0)
+    scale = jnp.where(order == 0, 1.0, 2.0)
+    scaled = jnp.where(morder[...].reshape(1, MODES) == order, scale, 0.0).astype(BF)
+    moved = jnp.where(order == ROWS * (lane & (NL - 1)) + (lane >> 6), 1.0, 0.0).astype(BF)
+    scaled = dot(scaled, moved).astype(BF)
     for reim in range(2):
-        itab[:, reim * MODES : (reim + 1) * MODES] = dot(twt_v[reim], hot).astype(BF)
+        itab[:, reim * MODES : (reim + 1) * MODES] = dot(twt_v[reim], scaled).astype(BF)
     loads[6].wait()
     loads[7].wait()
 
@@ -324,10 +331,9 @@
             ]
             eq[g] = jnp.concatenate(tiles, axis=1).astype(BF)
 
-    def pack_halves(backs):
-        for h in range(2):
-            tiles = [gather(backs[i], 4 * h, 4) for i in range(2)]
-            eh[h] = jnp.concatenate(tiles, axis=1).astype(BF)
+    def pack_half(backs, h):
+        tiles = [gather(backs[i], 4 * h, 4) for i in range(2)]
+        eh[h] = jnp.concatenate(tiles, axis=1).astype(BF)
 
     def send_quarter(g):
         lat_send(eq.at[g], rq.at[g], q_snd.at[g], q_rcv.at[g])
@@ -392,9 +398,11 @@
     backs.append(synthesise(3, received(3)))
     pack_quarters(backs)
     send_quarter(0)
-    pack_halves([synthesise(k, filtered(k)) for k in (4, 5)])
+    backs = [synthesise(k, filtered(k)) for k in (4, 5)]
+    pack_half(backs, 0)
     send_half(0)
     send_quarter(1)
+    pack_half(backs, 1)
     send_half(1)
     send_quarter(2)
     send_quarter(3)

time: 111 us -> 111 us (level)
  no operation moved by 1% of the time
where the time goes in v7:
time: 111 us
  Pallas kernels  111 us (100%)
    pallas_call x1, Pallas kernels, body(): pl.pallas_call(kernel, out_shape=jax.ShapeDtypeStruct((CYC // 2, 2 * LON,...  108 us
    pallas_call x1, Pallas kernels, body(): pl.pallas_call(finish, out_shape=jax.ShapeDtypeStruct(part.shape, BF), in...  2.78 us

profile of v7, /device:TPU:1, one launch (start us, length us, event | category | flops | bytes accessed | tf_op | source)
XLA Modules:
  0.0 110.8 jit_solution(17885984929992934322)
XLA Ops:
  0.0 107.8 %sfno_block.1.part_h = bf16[4,720,512]{2,1,0:T(8,128)(2,1)} custom-call(s32[384]{0:T(512)} %morder.1, f32[1,512]{1,0:T(1,128)} %bitcast.5, f32[1,512]{1,0:T(1,128)} %bitcast.6, f32[1,1024]{1,0:T(1,128)} %bitcast.4, bf16[8,1440,128]{2,1,0:T(8,128)(2,1)} %grid_h.1, bf16[2,384,1440]{2,1,0:T(8,128)(2,1)} %constant.4.clone.tw_h, ...), custom_call_target="tpu_custom_call" | custom-call | tf_op jit(solution)/shard_map/sfno_block/pallas_call | solution.py:453
  107.8 2.8 %move_result.1 = bf16[4,720,512]{2,1,0:T(8,128)(2,1)} custom-call(bf16[4,720,512]{2,1,0:T(8,128)(2,1)} %sfno_block.1.part_h), custom_call_target="tpu_custom_call" | custom-call | tf_op jit(solution)/shard_map/move_result/pallas_call | solution.py:526

commit v8 on v6

--- a/solution.py
+++ b/solution.py
@@ -357,18 +357,19 @@
             gs[p, i] = jnp.concatenate(
                 [b[i * LON : (i + 1) * LON] for b in both], axis=0
             ).astype(BF)
-        for t, (pair, at, n) in enumerate(PIECES):
-            if pair == p:
-                part = pl.ds(at, n)
-                ch_send(
-                    lambda i: gs.at[p, i, part], gr.at[p, x, part], g_snd.at[t], g_rcv.at[t]
-                )
-
-
-    def points(t):
+        send_piece(p)
+
+    def send_piece(t):
+        p, at, n = PIECES[t]
+        part = pl.ds(at, n)
+        ch_send(lambda i: gs.at[p, i, part], gr.at[p, x, part], g_snd.at[t], g_rcv.at[t])
+
+    def points(t, follow=None):
         p, at, n = PIECES[t]
         part = pl.ds(at, n)
         take(gr.at[p, :, part], g_rcv.at[t])
+        if follow is not None:
+            send_piece(follow)
         rows = jnp.concatenate([gr[p, i, part, :] for i in range(NX)], axis=1)
         ov[p, part, :] = point_layer(rows, lng, win_v, bias, wout_v)
         copy = pltpu.make_async_copy(ov.at[p, part], out_h.at[p, part], o_sem.at[t])
@@ -405,7 +406,10 @@
     copies = [points(0)]
     waves(2)
     waves(3)
-    copies += [points(t) for t in range(1, len(PIECES))]
+    copies.append(points(1))
+    send_piece(4)
+    copies.append(points(2, 5))
+    copies += [points(t) for t in range(3, len(PIECES))]
 
     for k in range(ROWS):
         take(sbuf.at[k, pl.ds(0, NL - 1)], s_snd.at[k])

time: 111 us -> 111 us (level)
  no operation moved by 1% of the time
where the time goes in v8:
time: 111 us; the launch traced here: 110 us
  Pallas kernels  110 us (99%)
    pallas_call x1, Pallas kernels, body(): pl.pallas_call(kernel, out_shape=jax.ShapeDtypeStruct((CYC // 2, 2 * LON,...  107 us
    pallas_call x1, Pallas kernels, body(): pl.pallas_call(finish, out_shape=jax.ShapeDtypeStruct(part.shape, BF), in...  2.78 us

profile of v8, /device:TPU:1, one launch (start us, length us, event | category | flops | bytes accessed | tf_op | source)
XLA Modules:
  0.0 110.5 jit_solution(10370777052484270911)
XLA Ops:
  0.0 107.5 %sfno_block.1.part_h = bf16[4,720,512]{2,1,0:T(8,128)(2,1)} custom-call(s32[384]{0:T(512)} %morder.1, f32[1,512]{1,0:T(1,128)} %bitcast.5, f32[1,512]{1,0:T(1,128)} %bitcast.6, f32[1,1024]{1,0:T(1,128)} %bitcast.4, bf16[8,1440,128]{2,1,0:T(8,128)(2,1)} %grid_h.1, bf16[2,384,1440]{2,1,0:T(8,128)(2,1)} %constant.4.clone.tw_h, ...), custom_call_target="tpu_custom_call" | custom-call | tf_op jit(solution)/shard_map/sfno_block/pallas_call | solution.py:449
  107.5 2.8 %move_result.1 = bf16[4,720,512]{2,1,0:T(8,128)(2,1)} custom-call(bf16[4,720,512]{2,1,0:T(8,128)(2,1)} %sfno_block.1.part_h), custom_call_target="tpu_custom_call" | custom-call | tf_op jit(solution)/shard_map/move_result/pallas_call | solution.py:522

commit v9 on v8

--- a/solution.py
+++ b/solution.py
@@ -20,7 +20,7 @@
 LQ = NL // NX
 LON = NLON // NX
 KP = ROWS // 2
-PIECES = [(0, 0, 720), (1, 0, 720), (2, 0, 720), (3, 0, 256), (3, 256, 256), (3, 512, 208)]
+PIECES = [(0, 0, 720), (1, 0, 720), (2, 0, 720), (3, 0, 240), (3, 240, 240), (3, 480, 240)]
 MESH = pl.DeviceIdType.MESH
 BF = jnp.bfloat16
 F32 = jnp.float32
@@ -208,7 +208,8 @@
         table = jnp.concatenate(
             [dot(rows, tw_v[0]).astype(BF), dot(rows, tw_v[1]).astype(BF)], axis=0
         )
-        for p in range(CYC // 2):
+        @pl.loop(0, CYC // 2)
+        def _(p):
             res = dot(table, jnp.concatenate([grid_v[2 * p], grid_v[2 * p + 1]], axis=1))
             for reim in range(2):
                 for k2 in range(2):
@@ -218,6 +219,7 @@
                         stage[pl.ds(row, NL, stride=16), :] = res[
                             at : at + NL, c * CB : (c + 1) * CB
                         ]
+
         for k2 in range(2):
             part = stage[k2 * NL * 16 : (k2 + 1) * NL * 16]
             sbuf[2 * kp + k2] = part.astype(BF).reshape(NL, 16, CB)
@@ -370,8 +372,13 @@
         take(gr.at[p, :, part], g_rcv.at[t])
         if follow is not None:
             send_piece(follow)
-        rows = jnp.concatenate([gr[p, i, part, :] for i in range(NX)], axis=1)
-        ov[p, part, :] = point_layer(rows, lng, win_v, bias, wout_v)
+
+        @pl.loop(0, n // 240)
+        def _(b):
+            block = pl.ds(pl.multiple_of(at + b * 240, 16), 240)
+            rows = jnp.concatenate([gr[p, i, block, :] for i in range(NX)], axis=1)
+            ov[p, block, :] = point_layer(rows, lng, win_v, bias, wout_v)
+
         copy = pltpu.make_async_copy(ov.at[p, part], out_h.at[p, part], o_sem.at[t])
         copy.start()
         return copy

time: 111 us -> 112 us (level)
  Pallas kernels: 110 us -> 112 us
    pallas_call x1, Pallas kernels: 107 us -> 109 us  [body(): pl.pallas_call(kernel, out_shape=jax.ShapeDtypeStruct((CYC // 2, 2 * LON,...]
where the time goes in v9:
time: 112 us
  Pallas kernels  112 us (100%)
    pallas_call x1, Pallas kernels, body(): pl.pallas_call(kernel, out_shape=jax.ShapeDtypeStruct((CYC // 2, 2 * LON,...  109 us
    pallas_call x1, Pallas kernels, body(): pl.pallas_call(finish, out_shape=jax.ShapeDtypeStruct(part.shape, BF), in...  2.78 us

profile of v9, /device:TPU:1, one launch (start us, length us, event | category | flops | bytes accessed | tf_op | source)
XLA Modules:
  0.0 112.1 jit_solution(7396221824896341340)
XLA Ops:
  0.0 109.1 %sfno_block.1.part_h = bf16[4,720,512]{2,1,0:T(8,128)(2,1)} custom-call(s32[384]{0:T(512)} %morder.1, f32[1,512]{1,0:T(1,128)} %bitcast.5, f32[1,512]{1,0:T(1,128)} %bitcast.6, f32[1,1024]{1,0:T(1,128)} %bitcast.4, bf16[8,1440,128]{2,1,0:T(8,128)(2,1)} %grid_h.1, bf16[2,384,1440]{2,1,0:T(8,128)(2,1)} %constant.4.clone.tw_h, ...), custom_call_target="tpu_custom_call" | custom-call | tf_op jit(solution)/shard_map/sfno_block/pallas_call | solution.py:456
  109.1 2.8 %move_result.1 = bf16[4,720,512]{2,1,0:T(8,128)(2,1)} custom-call(bf16[4,720,512]{2,1,0:T(8,128)(2,1)} %sfno_block.1.part_h), custom_call_target="tpu_custom_call" | custom-call | tf_op jit(solution)/shard_map/move_result/pallas_call | solution.py:529
